TPU v7x, 1024 devices: a whole 4x4x32 slice. The times are simulated.
1024 devices in a mesh: grp: 4 (over y), dom: 64 (over z, core), lev: 4 (over x).
Axes of the slice: x: 4, y: 4, z: 32, core: 2. Of those that a mesh axis runs over, the one named last changes fastest.
Arguments:
- atm_surface: bfloat16 [12, 1048576], P('lev', ('grp', 'dom')), may hold values from -12 to 12
- atm_levels: bfloat16 [80, 1048576], P('lev', ('grp', 'dom')), may hold values from -12 to 12
- margin_weights: bfloat16 [256, 8, 64, 2048], P(('grp', 'dom')), may hold values from 0 to 0.0625
- src_block: int32 [256, 8, 32], P(('grp', 'dom')), may hold values from 0 to 63
- dst_block: int32 [256, 8, 32], P(('grp', 'dom')), may hold values from -1 to 31, as said below
- ice_cover: float32 [524288], P(('grp', 'dom')), may hold values from 0 to 1
- ice_flux: bfloat16 [12, 524288], P('lev', ('grp', 'dom')), may hold values from -6 to 6
- ocean_state: bfloat16 [12, 524288], P('lev', ('grp', 'dom')), may hold values from -6 to 6
- drag: float32 [524288], P(('grp', 'dom')), may hold values from 0.5 to 2
- level_weights: float32 [80], P('lev'), may hold values from 0.025 to 0.225
- neighbours: int32 [524288, 6], P(('grp', 'dom')), may hold values from 0 to 2303, as said below
Outputs:
- ocean_surface: float32 [12, 524288], P('lev', ('grp', 'dom'))
- ocean_levels: float32 [80, 524288], P('lev', ('grp', 'dom'))
- atm_flux: float32 [12, 1048576], P('lev', ('grp', 'dom'))
Inputs may be any that keep to these rules, and one draw needn't show every extreme that they name: `dst_block`: -1 marks an unused slot. `neighbours`: entry e names the partition's cell e - 128, counted from the partition's first cell, so values below 128 reach into the previous partition of the region group and values of 2176 or more into the next.
All inputs are finite; a program needn't handle non-finite values.
Results may differ from a plain program's by a relative error of at most 0.0034.
Values may be sent and summed in bfloat16 or wider, within the bound.
A program may use at most 64 MiB of HBM per device.

v0:
```python
import jax
import jax.numpy as jnp
from jax import lax
from jax.sharding import PartitionSpec as P

HW = 128


KAPPA = 0.5


def from_behind(x, axis, by):
    devices = lax.axis_size(axis)
    return lax.ppermute(x, axis, [(i, (i + by) % devices) for i in range(devices)])


def extended_2(cells, sides, width):
    for axis, dim in sides:
        count = lax.axis_size(axis)
        head = lax.slice_in_dim(cells, 0, width, axis=dim)
        tail = lax.slice_in_dim(cells, cells.shape[dim] - width, cells.shape[dim], axis=dim)
        cells = jnp.concatenate(
            [
                lax.ppermute(tail, axis, [(i, (i + 1) % count) for i in range(count)]),
                cells,
                lax.ppermute(head, axis, [((i + 1) % count, i) for i in range(count)]),
            ],
            axis=dim,
        )
    return cells


def shards(
    atm_surface,
    atm_levels,
    margin_weights,
    src_block,
    dst_block,
    ice_cover,
    ice_flux,
    ocean_state,
    drag,
    level_weights,
    neighbours,
):
    surf_dev = atm_surface.shape[0]
    fields = jnp.concatenate([atm_surface, atm_levels], axis=0)
    chans = fields.shape[0]
    near = margin_weights.shape[1]
    width = margin_weights.shape[2]
    slots = src_block.shape[2]
    src_count = fields.shape[1] // width
    own_cells = ice_cover.shape[0]
    tgt_count = own_cells // width
    weight_mat = margin_weights[0].reshape(near, width, slots, width)
    src_ids = src_block[0]
    dst_ids = dst_block[0]
    picked = jnp.take(fields.reshape(chans, src_count, width), src_ids.reshape(-1), axis=1)
    picked = picked.reshape(chans, near, slots, width)
    pieces = jnp.einsum("kdci,dicj->dkcj", picked, weight_mat, preferred_element_type=jnp.float32)
    outgoing = pieces.astype(jnp.bfloat16).reshape(near, chans, slots * width)
    moved_pieces = [outgoing[0]]
    moved_ids = [dst_ids[0]]
    for offset in range(1, near):
        got_pieces, got_ids = from_behind(
            (outgoing[offset], dst_ids[offset]), ("grp", "dom"), offset
        )
        moved_pieces.append(got_pieces)
        moved_ids.append(got_ids)
    arrived = jnp.stack(moved_pieces, axis=0)
    arrived_ids = jnp.stack(moved_ids, axis=0)
    block_iota = jnp.arange(tgt_count, dtype=jnp.int32)
    selector = (arrived_ids[..., None] == block_iota).astype(jnp.bfloat16)
    remapped = jnp.einsum(
        "okcj,oct->ktj",
        arrived.reshape(near, chans, slots, width),
        selector,
        preferred_element_type=jnp.float32,
    ).reshape(chans, own_cells)
    ice_share = ice_cover[None, :]
    surface = (1.0 - ice_share) * remapped[:surf_dev] + ice_share * ice_flux.astype(jnp.float32)
    merged = jnp.concatenate([surface, remapped[surf_dev:]], axis=0).astype(jnp.bfloat16)
    extended = extended_2(merged, (("dom", 1),), HW)
    nearby = jnp.take(extended, neighbours.reshape(-1), axis=1).reshape(
        chans, own_cells, neighbours.shape[1]
    )
    beside_all = jnp.sum(nearby.astype(jnp.float32), axis=2) / neighbours.shape[1]
    centre = merged.astype(jnp.float32)
    forcing = centre + KAPPA * (beside_all - centre)
    column = lax.psum(jnp.sum(level_weights[:, None] * forcing[surf_dev:], axis=0), "lev")
    flux = (
        drag[None, :] * (ocean_state.astype(jnp.float32) - forcing[:surf_dev] + column[None, :])
    ).astype(jnp.bfloat16)
    flux_blocks = flux.reshape(surf_dev, tgt_count, width)
    picked_back = jnp.einsum(
        "oct,stj->ocsj", selector, flux_blocks, preferred_element_type=jnp.float32
    ).astype(jnp.bfloat16)
    back_list = [picked_back[0]]
    for offset in range(1, near):
        back_list.append(from_behind(picked_back[offset], ("grp", "dom"), -offset))
    returned = jnp.stack(back_list, axis=0)
    spread = jnp.einsum("ocsj,oicj->ocsi", returned, weight_mat, preferred_element_type=jnp.float32)
    owner = (src_ids[..., None] == jnp.arange(src_count, dtype=jnp.int32)).astype(jnp.float32)
    atm_back = jnp.einsum("ocsi,ocb->sbi", spread, owner, precision=lax.Precision.HIGHEST)
    return (forcing[:surf_dev], forcing[surf_dev:], atm_back.reshape(surf_dev, src_count * width))


def solution(mesh):
    return jax.shard_map(
        shards,
        mesh=mesh,
        in_specs=(
            P("lev", ("grp", "dom")),
            P("lev", ("grp", "dom")),
            P(("grp", "dom"), None, None, None),
            P(("grp", "dom"), None, None),
            P(("grp", "dom"), None, None),
            P(("grp", "dom")),
            P("lev", ("grp", "dom")),
            P("lev", ("grp", "dom")),
            P(("grp", "dom")),
            P("lev"),
            P(("grp", "dom"), None),
        ),
        out_specs=(P("lev", ("grp", "dom")), P("lev", ("grp", "dom")), P("lev", ("grp", "dom"))),
        check_vma=False,
    )
```

profile of v0, /device:TPU:1, one launch (start us, length us, event | category | flops | bytes accessed | tf_op | source)
XLA Modules:
  0.0 220.4 jit_solution(16954489125383021969)
XLA Ops:
  2.1 7.1 %reshape_squeeze.10 = bf16[8,64,32,64]{3,2,1,0:T(8,128)(2,1)} reshape(bf16[1,8,64,2048]{3,2,1,0:T(8,128)(2,1)} %param.13) | data formatting | bytes 4194304 | tf_op jit(solution)/shard_map/reshape;squeeze | solution.py:55
  10.9 4.1 %fusion.11 = bf16[8,23,32,64]{3,1,2,0:T(8,128)(2,1)S(1)} fusion(bf16[8,64,32,64]{3,2,1,0:T(8,128)(2,1)} %reshape_squeeze.10, bf16[23,8,32,64]{3,0,2,1:T(8,128)(2,1)S(1)} %bitcast.102, pred[8,32]{1,0:T(8,128)(4,1)S(1)} %compare_and_fusion.1), kind=kOutput, calls=%fused_computation.12 | convolution fusion | flops 48988160 | bytes 3604736 | tf_op jit(solution)/shard_map/kdci,dicj->dkcj/dot_general | solution.py:60
  16.2 4.9 %collective-permute-start.7 = (bf16[23,2048]{1,0:T(8,128)(2,1)}, bf16[23,2048]{1,0:T(8,128)(2,1)}, u32[]{:S(2)}, u32[]{:S(2)}) collective-permute-start(bf16[23,2048]{1,0:T(8,128)(2,1)} %squeeze.71), channel_id=1, source_target_pairs={{0,4},{4,8},{8,12},{12,16},{16,20},{20,24},{24,28},{28,32},{32,36}... | collective-permute-start | bytes 282632 | tf_op jit(solution)/shard_map/ppermute | solution.py:14
  22.0 3.7 %collective-permute-start.8 = (bf16[23,2048]{1,0:T(8,128)(2,1)}, bf16[23,2048]{1,0:T(8,128)(2,1)}, u32[]{:S(2)}, u32[]{:S(2)}) collective-permute-start(bf16[23,2048]{1,0:T(8,128)(2,1)} %squeeze.72), channel_id=1, source_target_pairs={{0,8},{4,12},{8,16},{12,20},{16,24},{20,28},{24,32},{28,36},{32,40... | collective-permute-start | bytes 282632 | tf_op jit(solution)/shard_map/ppermute | solution.py:14
  26.5 3.5 %collective-permute-start.9 = (bf16[23,2048]{1,0:T(8,128)(2,1)}, bf16[23,2048]{1,0:T(8,128)(2,1)}, u32[]{:S(2)}, u32[]{:S(2)}) collective-permute-start(bf16[23,2048]{1,0:T(8,128)(2,1)} %squeeze.73), channel_id=1, source_target_pairs={{0,12},{4,16},{8,20},{12,24},{16,28},{20,32},{24,36},{28,40},{32,4... | collective-permute-start | bytes 282632 | tf_op jit(solution)/shard_map/ppermute | solution.py:14
  30.6 7.7 %collective-permute-start.4 = (s32[32]{0:T(128)}, s32[32]{0:T(128)S(1)}, u32[]{:S(2)}, u32[]{:S(2)}) collective-permute-start(s32[32]{0:T(128)} %get-tuple-element.38), channel_id=1, source_target_pairs={{0,20},{4,24},{8,28},{12,32},{16,36},{20,40},{24,44},{28,48},{32,5... | collective-permute-start | bytes 392 | tf_op jit(solution)/shard_map/ppermute | solution.py:14
  38.3 7.5 %collective-permute-start.5 = (s32[32]{0:T(128)}, s32[32]{0:T(128)S(1)}, u32[]{:S(2)}, u32[]{:S(2)}) collective-permute-start(s32[32]{0:T(128)} %get-tuple-element.44), channel_id=1, source_target_pairs={{0,24},{4,28},{8,32},{12,36},{16,40},{20,44},{24,48},{28,52},{32,5... | collective-permute-start | bytes 392 | tf_op jit(solution)/shard_map/ppermute | solution.py:14
  49.4 6.4 %collective-permute-start.6 = (s32[32]{0:T(128)S(1)}, s32[32]{0:T(128)S(1)}, u32[]{:S(2)}, u32[]{:S(2)}) collective-permute-start(s32[32]{0:T(128)S(1)} %copy-done.11), channel_id=1, source_target_pairs={{0,28},{4,32},{8,36},{12,40},{16,44},{20,48},{24,52},{28,56},{32,6... | collective-permute-start | bytes 392 | tf_op jit(solution)/shard_map/ppermute | solution.py:14
  59.4 3.5 %collective-permute-start.1 = (s32[32]{0:T(128)S(1)}, s32[32]{0:T(128)S(1)}, u32[]{:S(2)}, u32[]{:S(2)}) collective-permute-start(s32[32]{0:T(128)S(1)} %get-tuple-element.41), channel_id=1, source_target_pairs={{0,8},{4,12},{8,16},{12,20},{16,24},{20,28},{24,32},{28,36},{32,40... | collective-permute-start | bytes 392 | tf_op jit(solution)/shard_map/ppermute | solution.py:14
  62.9 3.9 %collective-permute-start.2 = (s32[32]{0:T(128)S(1)}, s32[32]{0:T(128)S(1)}, u32[]{:S(2)}, u32[]{:S(2)}) collective-permute-start(s32[32]{0:T(128)S(1)} %get-tuple-element.40), channel_id=1, source_target_pairs={{0,12},{4,16},{8,20},{12,24},{16,28},{20,32},{24,36},{28,40},{32,4... | collective-permute-start | bytes 392 | tf_op jit(solution)/shard_map/ppermute | solution.py:14
  67.0 5.9 %collective-permute-start.3 = (s32[32]{0:T(128)S(1)}, s32[32]{0:T(128)S(1)}, u32[]{:S(2)}, u32[]{:S(2)}) collective-permute-start(s32[32]{0:T(128)S(1)} %get-tuple-element.39), channel_id=1, source_target_pairs={{0,16},{4,20},{8,24},{12,28},{16,32},{20,36},{24,40},{28,44},{32,4... | collective-permute-start | bytes 392 | tf_op jit(solution)/shard_map/ppermute | solution.py:14
  75.5 5.0 %collective-permute-start.11 = (bf16[23,2048]{1,0:T(8,128)(2,1)S(1)}, bf16[23,2048]{1,0:T(8,128)(2,1)S(1)}, u32[]{:S(2)}, u32[]{:S(2)}) collective-permute-start(bf16[23,2048]{1,0:T(8,128)(2,1)S(1)} %squeeze.75), channel_id=1, source_target_pairs={{0,20},{4,24},{8,28},{12,32},{16,36},{20,40},{24,44},{28,48},{32,5... | collective-permute-start | bytes 282632 | tf_op jit(solution)/shard_map/ppermute | solution.py:14
  80.6 5.2 %collective-permute-start.12 = (bf16[23,2048]{1,0:T(8,128)(2,1)S(1)}, bf16[23,2048]{1,0:T(8,128)(2,1)S(1)}, u32[]{:S(2)}, u32[]{:S(2)}) collective-permute-start(bf16[23,2048]{1,0:T(8,128)(2,1)S(1)} %squeeze.76), channel_id=1, source_target_pairs={{0,24},{4,28},{8,32},{12,36},{16,40},{20,44},{24,48},{28,52},{32,5... | collective-permute-start | bytes 282632 | tf_op jit(solution)/shard_map/ppermute | solution.py:14
  96.6 7.8 %collective-permute-done.13 = bf16[23,2048]{1,0:T(8,128)(2,1)S(1)} collective-permute-done((bf16[23,2048]{1,0:T(8,128)(2,1)S(1)}, bf16[23,2048]{1,0:T(8,128)(2,1)S(1)}, u32[]{:S(2)}, u32[]{:S(2)}) %collective-permute-start.13) | collective-permute-done | bytes 94240 | tf_op jit(solution)/shard_map/ppermute | solution.py:14
  109.8 43.6 %gather_fusion.1 = bf16[12288,23]{1,0:T(8,128)(2,1)} fusion(bf16[23,2304]{0,1:T(8,128)(2,1)S(1)} %copy.158, s32[12288]{0:T(1024)S(1)} %broadcast_clamp_fusion), kind=kCustom, calls=%fused_computation.1 | custom fusion | bytes 1179648 | tf_op jit(solution)/shard_map/jit(_take)/gather | solution.py:84
  153.4 6.8 %gather.15 = bf16[23,2048,6]{0,2,1:T(8,128)(2,1)} reshape(bf16[23,12288]{0,1:T(8,128)(2,1)} %bitcast.101) | data formatting | bytes 1130496 | tf_op jit(solution)/shard_map/jit(_take)/gather | solution.py:84
  160.1 12.8 %convert_reduce_fusion = f32[23,2048]{0,1:T(8,128)S(1)} fusion(bf16[23,2048,6]{0,2,1:T(8,128)(2,1)} %gather.15, pred[2048,6]{1,0:T(8,128)(4,1)S(1)} %copy.156), kind=kLoop, calls=%fused_computation.2 | loop fusion | flops 800768 | bytes 765952 | tf_op jit(solution)/shard_map/reduce_sum | solution.py:87
  174.3 8.6 %psum.7 = f32[2048]{0:T(1024)S(1)} all-reduce(f32[2048]{0:T(1024)S(1)} %get-tuple-element.17), channel_id=1, replica_groups=mesh['grp'=4,'dom'=64,'lev'=4] {'lev'}, use_global_device_ids=true, to_apply=%region_2.3 | all-reduce | flops 2048 | bytes 16384 | tf_op jit(solution)/shard_map/psum | solution.py:90
  184.0 4.4 %collective-permute-start.16 = (bf16[32,3,64]{2,0,1:T(8,128)(2,1)S(1)}, bf16[32,3,64]{2,0,1:T(8,128)(2,1)S(1)}, u32[]{:S(2)}, u32[]{:S(2)}) collective-permute-start(bf16[32,3,64]{2,0,1:T(8,128)(2,1)S(1)} %get-tuple-element.33), channel_id=1, source_target_pairs={{0,1020},{4,0},{8,4},{12,8},{16,12},{20,16},{24,20},{28,24},{32,28... | collective-permute-start | bytes 36872 | tf_op jit(solution)/shard_map/ppermute | solution.py:14
  193.5 5.1 %collective-permute-start.19 = (bf16[32,3,64]{2,0,1:T(8,128)(2,1)S(1)}, bf16[32,3,64]{2,0,1:T(8,128)(2,1)S(1)}, u32[]{:S(2)}, u32[]{:S(2)}) collective-permute-start(bf16[32,3,64]{2,0,1:T(8,128)(2,1)S(1)} %get-tuple-element.30), channel_id=1, source_target_pairs={{0,1008},{4,1012},{8,1016},{12,1020},{16,0},{20,4},{24,8},{28,12},... | collective-permute-start | bytes 36872 | tf_op jit(solution)/shard_map/ppermute | solution.py:14
  200.6 4.4 %collective-permute-start.21 = (bf16[32,3,64]{2,0,1:T(8,128)(2,1)S(1)}, bf16[32,3,64]{2,0,1:T(8,128)(2,1)S(1)}, u32[]{:S(2)}, u32[]{:S(2)}) collective-permute-start(bf16[32,3,64]{2,0,1:T(8,128)(2,1)S(1)} %get-tuple-element.28), channel_id=1, source_target_pairs={{0,1000},{4,1004},{8,1008},{12,1012},{16,1016},{20,1020},{24,0},{2... | collective-permute-start | bytes 36872 | tf_op jit(solution)/shard_map/ppermute | solution.py:14
  205.1 4.9 %collective-permute-start.22 = (bf16[32,3,64]{2,0,1:T(8,128)(2,1)S(1)}, bf16[32,3,64]{2,0,1:T(8,128)(2,1)S(1)}, u32[]{:S(2)}, u32[]{:S(2)}) collective-permute-start(bf16[32,3,64]{2,0,1:T(8,128)(2,1)S(1)} %get-tuple-element.27), channel_id=1, source_target_pairs={{0,996},{4,1000},{8,1004},{12,1008},{16,1012},{20,1016},{24,1020},... | collective-permute-start | bytes 36872 | tf_op jit(solution)/shard_map/ppermute | solution.py:14
  210.1 4.7 %collective-permute-done.22 = bf16[32,3,64]{2,0,1:T(8,128)(2,1)S(1)} collective-permute-done((bf16[32,3,64]{2,0,1:T(8,128)(2,1)S(1)}, bf16[32,3,64]{2,0,1:T(8,128)(2,1)S(1)}, u32[]{:S(2)}, u32[]{:S(2)}) %collective-permute-start.22) | collective-permute-done | bytes 12320 | tf_op jit(solution)/shard_map/ppermute | solution.py:14
  214.8 4.5 %fusion = f32[8,32,3,64]{3,2,1,0:T(4,128)S(1)} fusion(bf16[8,64,32,64]{3,2,1,0:T(8,128)(2,1)} %reshape_squeeze.10, bf16[8,32,3,64]{3,1,2,0:T(8,128)(2,1)S(1)} %constant_dynamic-update-slice_fusion), kind=kOutput, calls=%fused_computation.3 | convolution fusion | flops 6291456 | bytes 2392064 | tf_op jit(solution)/shard_map/ocsj,oicj->ocsi/dot_general | solution.py:102
  (124 shorter events, 42.9 us)
Async XLA Ops:
  15.3 30.5 %copy-start = (s32[2048,6]{0,1:T(8,128)S(1)}, s32[2048,6]{0,1:T(8,128)}, u32[]{:S(2)}) copy-start(s32[2048,6]{0,1:T(8,128)} %param.21) | copy-start | bytes 147460
  16.2 64.5 %collective-permute-start.7 = (bf16[23,2048]{1,0:T(8,128)(2,1)}, bf16[23,2048]{1,0:T(8,128)(2,1)}, u32[]{:S(2)}, u32[]{:S(2)}) collective-permute-start(bf16[23,2048]{1,0:T(8,128)(2,1)} %squeeze.71), channel_id=1, source_target_pairs={{0,4},{4,8},{8,12},{12,16},{16,20},{20,24},{24,28},{28,32},{32,36}... | collective-permute-start | bytes 282632 | tf_op jit(solution)/shard_map/ppermute | solution.py:14
  22.0 65.1 %collective-permute-start.8 = (bf16[23,2048]{1,0:T(8,128)(2,1)}, bf16[23,2048]{1,0:T(8,128)(2,1)}, u32[]{:S(2)}, u32[]{:S(2)}) collective-permute-start(bf16[23,2048]{1,0:T(8,128)(2,1)} %squeeze.72), channel_id=1, source_target_pairs={{0,8},{4,12},{8,16},{12,20},{16,24},{20,28},{24,32},{28,36},{32,40... | collective-permute-start | bytes 282632 | tf_op jit(solution)/shard_map/ppermute | solution.py:14
  26.5 65.2 %collective-permute-start.9 = (bf16[23,2048]{1,0:T(8,128)(2,1)}, bf16[23,2048]{1,0:T(8,128)(2,1)}, u32[]{:S(2)}, u32[]{:S(2)}) collective-permute-start(bf16[23,2048]{1,0:T(8,128)(2,1)} %squeeze.73), channel_id=1, source_target_pairs={{0,12},{4,16},{8,20},{12,24},{16,28},{20,32},{24,36},{28,40},{32,4... | collective-permute-start | bytes 282632 | tf_op jit(solution)/shard_map/ppermute | solution.py:14
  30.6 18.8 %collective-permute-start.4 = (s32[32]{0:T(128)}, s32[32]{0:T(128)S(1)}, u32[]{:S(2)}, u32[]{:S(2)}) collective-permute-start(s32[32]{0:T(128)} %get-tuple-element.38), channel_id=1, source_target_pairs={{0,20},{4,24},{8,28},{12,32},{16,36},{20,40},{24,44},{28,48},{32,5... | collective-permute-start | bytes 392 | tf_op jit(solution)/shard_map/ppermute | solution.py:14
  38.3 17.5 %collective-permute-start.5 = (s32[32]{0:T(128)}, s32[32]{0:T(128)S(1)}, u32[]{:S(2)}, u32[]{:S(2)}) collective-permute-start(s32[32]{0:T(128)} %get-tuple-element.44), channel_id=1, source_target_pairs={{0,24},{4,28},{8,32},{12,36},{16,40},{20,44},{24,48},{28,52},{32,5... | collective-permute-start | bytes 392 | tf_op jit(solution)/shard_map/ppermute | solution.py:14
  49.4 10.0 %collective-permute-start.6 = (s32[32]{0:T(128)S(1)}, s32[32]{0:T(128)S(1)}, u32[]{:S(2)}, u32[]{:S(2)}) collective-permute-start(s32[32]{0:T(128)S(1)} %copy-done.11), channel_id=1, source_target_pairs={{0,28},{4,32},{8,36},{12,40},{16,44},{20,48},{24,52},{28,56},{32,6... | collective-permute-start | bytes 392 | tf_op jit(solution)/shard_map/ppermute | solution.py:14
  55.8 7.1 %collective-permute-start = (s32[32]{0:T(128)S(1)}, s32[32]{0:T(128)S(1)}, u32[]{:S(2)}, u32[]{:S(2)}) collective-permute-start(s32[32]{0:T(128)S(1)} %copy-done.10), channel_id=1, source_target_pairs={{0,4},{4,8},{8,12},{12,16},{16,20},{20,24},{24,28},{28,32},{32,36}... | collective-permute-start | bytes 392 | tf_op jit(solution)/shard_map/ppermute | solution.py:14
  59.4 7.6 %collective-permute-start.1 = (s32[32]{0:T(128)S(1)}, s32[32]{0:T(128)S(1)}, u32[]{:S(2)}, u32[]{:S(2)}) collective-permute-start(s32[32]{0:T(128)S(1)} %get-tuple-element.41), channel_id=1, source_target_pairs={{0,8},{4,12},{8,16},{12,20},{16,24},{20,28},{24,32},{28,36},{32,40... | collective-permute-start | bytes 392 | tf_op jit(solution)/shard_map/ppermute | solution.py:14
  62.9 10.0 %collective-permute-start.2 = (s32[32]{0:T(128)S(1)}, s32[32]{0:T(128)S(1)}, u32[]{:S(2)}, u32[]{:S(2)}) collective-permute-start(s32[32]{0:T(128)S(1)} %get-tuple-element.40), channel_id=1, source_target_pairs={{0,12},{4,16},{8,20},{12,24},{16,28},{20,32},{24,36},{28,40},{32,4... | collective-permute-start | bytes 392 | tf_op jit(solution)/shard_map/ppermute | solution.py:14
  67.0 8.6 %collective-permute-start.3 = (s32[32]{0:T(128)S(1)}, s32[32]{0:T(128)S(1)}, u32[]{:S(2)}, u32[]{:S(2)}) collective-permute-start(s32[32]{0:T(128)S(1)} %get-tuple-element.39), channel_id=1, source_target_pairs={{0,16},{4,20},{8,24},{12,28},{16,32},{20,36},{24,40},{28,44},{32,4... | collective-permute-start | bytes 392 | tf_op jit(solution)/shard_map/ppermute | solution.py:14
  72.9 20.0 %collective-permute-start.10 = (bf16[23,2048]{1,0:T(8,128)(2,1)S(1)}, bf16[23,2048]{1,0:T(8,128)(2,1)S(1)}, u32[]{:S(2)}, u32[]{:S(2)}) collective-permute-start(bf16[23,2048]{1,0:T(8,128)(2,1)S(1)} %squeeze.74), channel_id=1, source_target_pairs={{0,16},{4,20},{8,24},{12,28},{16,32},{20,36},{24,40},{28,44},{32,4... | collective-permute-start | bytes 282632 | tf_op jit(solution)/shard_map/ppermute | solution.py:14
  75.5 17.7 %collective-permute-start.11 = (bf16[23,2048]{1,0:T(8,128)(2,1)S(1)}, bf16[23,2048]{1,0:T(8,128)(2,1)S(1)}, u32[]{:S(2)}, u32[]{:S(2)}) collective-permute-start(bf16[23,2048]{1,0:T(8,128)(2,1)S(1)} %squeeze.75), channel_id=1, source_target_pairs={{0,20},{4,24},{8,28},{12,32},{16,36},{20,40},{24,44},{28,48},{32,5... | collective-permute-start | bytes 282632 | tf_op jit(solution)/shard_map/ppermute | solution.py:14
  80.6 15.8 %collective-permute-start.12 = (bf16[23,2048]{1,0:T(8,128)(2,1)S(1)}, bf16[23,2048]{1,0:T(8,128)(2,1)S(1)}, u32[]{:S(2)}, u32[]{:S(2)}) collective-permute-start(bf16[23,2048]{1,0:T(8,128)(2,1)S(1)} %squeeze.76), channel_id=1, source_target_pairs={{0,24},{4,28},{8,32},{12,36},{16,40},{20,44},{24,48},{28,52},{32,5... | collective-permute-start | bytes 282632 | tf_op jit(solution)/shard_map/ppermute | solution.py:14
  87.0 17.4 %collective-permute-start.13 = (bf16[23,2048]{1,0:T(8,128)(2,1)S(1)}, bf16[23,2048]{1,0:T(8,128)(2,1)S(1)}, u32[]{:S(2)}, u32[]{:S(2)}) collective-permute-start(bf16[23,2048]{1,0:T(8,128)(2,1)S(1)} %squeeze.77), channel_id=1, source_target_pairs={{0,28},{4,32},{8,36},{12,40},{16,44},{20,48},{24,52},{28,56},{32,6... | collective-permute-start | bytes 282632 | tf_op jit(solution)/shard_map/ppermute | solution.py:14
  105.6 1.3 collective-permute-start.14
  106.1 3.3 %collective-permute-start.15 = (bf16[23,128]{1,0:T(8,128)(2,1)S(1)}, bf16[23,128]{1,0:T(8,128)(2,1)S(1)}, u32[]{:S(2)}, u32[]{:S(2)}) collective-permute-start(bf16[23,128]{1,0:T(8,128)(2,1)S(1)} %get-tuple-element.36), channel_id=1, source_target_pairs={{4,0},{8,4},{12,8},{16,12},{20,16},{24,20},{28,24},{32,28},{36,32}... | collective-permute-start | bytes 17672 | tf_op jit(solution)/shard_map/ppermute | solution.py:26
  184.0 16.6 %collective-permute-start.16 = (bf16[32,3,64]{2,0,1:T(8,128)(2,1)S(1)}, bf16[32,3,64]{2,0,1:T(8,128)(2,1)S(1)}, u32[]{:S(2)}, u32[]{:S(2)}) collective-permute-start(bf16[32,3,64]{2,0,1:T(8,128)(2,1)S(1)} %get-tuple-element.33), channel_id=1, source_target_pairs={{0,1020},{4,0},{8,4},{12,8},{16,12},{20,16},{24,20},{28,24},{32,28... | collective-permute-start | bytes 36872 | tf_op jit(solution)/shard_map/ppermute | solution.py:14
  188.3 16.7 %collective-permute-start.17 = (bf16[32,3,64]{2,0,1:T(8,128)(2,1)S(1)}, bf16[32,3,64]{2,0,1:T(8,128)(2,1)S(1)}, u32[]{:S(2)}, u32[]{:S(2)}) collective-permute-start(bf16[32,3,64]{2,0,1:T(8,128)(2,1)S(1)} %get-tuple-element.32), channel_id=1, source_target_pairs={{0,1016},{4,1020},{8,0},{12,4},{16,8},{20,12},{24,16},{28,20},{32,... | collective-permute-start | bytes 36872 | tf_op jit(solution)/shard_map/ppermute | solution.py:14
  191.6 18.4 %collective-permute-start.18 = (bf16[32,3,64]{2,0,1:T(8,128)(2,1)S(1)}, bf16[32,3,64]{2,0,1:T(8,128)(2,1)S(1)}, u32[]{:S(2)}, u32[]{:S(2)}) collective-permute-start(bf16[32,3,64]{2,0,1:T(8,128)(2,1)S(1)} %get-tuple-element.31), channel_id=1, source_target_pairs={{0,1012},{4,1016},{8,1020},{12,0},{16,4},{20,8},{24,12},{28,16},{3... | collective-permute-start | bytes 36872 | tf_op jit(solution)/shard_map/ppermute | solution.py:14
  193.5 16.5 %collective-permute-start.19 = (bf16[32,3,64]{2,0,1:T(8,128)(2,1)S(1)}, bf16[32,3,64]{2,0,1:T(8,128)(2,1)S(1)}, u32[]{:S(2)}, u32[]{:S(2)}) collective-permute-start(bf16[32,3,64]{2,0,1:T(8,128)(2,1)S(1)} %get-tuple-element.30), channel_id=1, source_target_pairs={{0,1008},{4,1012},{8,1016},{12,1020},{16,0},{20,4},{24,8},{28,12},... | collective-permute-start | bytes 36872 | tf_op jit(solution)/shard_map/ppermute | solution.py:14
  198.7 11.4 %collective-permute-start.20 = (bf16[32,3,64]{2,0,1:T(8,128)(2,1)S(1)}, bf16[32,3,64]{2,0,1:T(8,128)(2,1)S(1)}, u32[]{:S(2)}, u32[]{:S(2)}) collective-permute-start(bf16[32,3,64]{2,0,1:T(8,128)(2,1)S(1)} %get-tuple-element.29), channel_id=1, source_target_pairs={{0,1004},{4,1008},{8,1012},{12,1016},{16,1020},{20,0},{24,4},{28,8... | collective-permute-start | bytes 36872 | tf_op jit(solution)/shard_map/ppermute | solution.py:14
  200.6 9.5 %collective-permute-start.21 = (bf16[32,3,64]{2,0,1:T(8,128)(2,1)S(1)}, bf16[32,3,64]{2,0,1:T(8,128)(2,1)S(1)}, u32[]{:S(2)}, u32[]{:S(2)}) collective-permute-start(bf16[32,3,64]{2,0,1:T(8,128)(2,1)S(1)} %get-tuple-element.28), channel_id=1, source_target_pairs={{0,1000},{4,1004},{8,1008},{12,1012},{16,1016},{20,1020},{24,0},{2... | collective-permute-start | bytes 36872 | tf_op jit(solution)/shard_map/ppermute | solution.py:14
  205.1 9.8 %collective-permute-start.22 = (bf16[32,3,64]{2,0,1:T(8,128)(2,1)S(1)}, bf16[32,3,64]{2,0,1:T(8,128)(2,1)S(1)}, u32[]{:S(2)}, u32[]{:S(2)}) collective-permute-start(bf16[32,3,64]{2,0,1:T(8,128)(2,1)S(1)} %get-tuple-element.27), channel_id=1, source_target_pairs={{0,996},{4,1000},{8,1004},{12,1008},{16,1012},{20,1016},{24,1020},... | collective-permute-start | bytes 36872 | tf_op jit(solution)/shard_map/ppermute | solution.py:14
  (11 other events, 91.3 us)
where the time goes:
time: 222 us; the launch traced here: 220 us
  starting transfers between devices  93.4 us (42%)
  local copies, waits for them, and re-layouts  72.5 us (33%)
  waiting for transfers between devices  19.7 us (9%)
  other arithmetic  15.2 us (7%)
  matrix products  9.66 us (4%)
  blocking collectives  8.6 us (4%)
    ppermute x21, starting transfers between devices, from_behind(): lax.ppermute(x, axis, [(i, (i + by) % devices) for i in range(devices)])  92.9 us
    gather x2, local copies, waits for them, and re-layouts, shards(): jnp.take(extended, neighbours.reshape(-1), axis=1)  50.3 us
    ppermute x21, waiting for transfers between devices, from_behind(): lax.ppermute(x, axis, [(i, (i + by) % devices) for i in range(devices)])  17 us
    reduce_sum x1, other arithmetic, shards(): jnp.sum(nearby.astype(jnp.float32), axis=2) / neighbours.shape[1]  12.8 us
    psum x1, blocking collectives, shards(): lax.psum(jnp.sum(level_weights[:, None] * forcing[surf_dev:], axis=0), 'l...  8.6 us
    another operation x1, local copies, waits for them, and re-layouts, shards(): weight_mat = margin_weights[0].reshape(near, width, slots, width)  7.1 us
    dot_general x1, matrix products, shards(): jnp.einsum('ocsj,oicj->ocsi', returned, weight_mat, preferred_element_typ...  4.47 us
  transfers between devices with their start and end apart: 23, of which 7 were waited for; matrix products, arithmetic and copies ran while one was open for 4% of the time, Pallas kernels for 0%

commit v1 on v0

v1 whole, which is shorter than its diff:
```python
import functools

import jax
import jax.numpy as jnp
from jax import lax
from jax.experimental import pallas as pl
from jax.experimental.pallas import tpu as pltpu
from jax.sharding import PartitionSpec as P

HW = 128
KAPPA = 0.5
ROWS = 24
MESH = pl.DeviceIdType.MESH
F32 = jnp.float32
BF16 = jnp.bfloat16


def dot(a, b):
    return jnp.dot(a, b, preferred_element_type=F32)


def forward_kernel(src, dst, surf_ref, lev_ref, w_ref, out_ref, joint, blocks, even, odd):
    o = pl.program_id(0)
    levels, surf = lev_ref.shape[0], surf_ref.shape[0]
    width = w_ref.shape[2]
    slots = w_ref.shape[3] // width
    count = even.shape[0] - 1

    @pl.when(o == 0)
    def _():
        joint[...] = jnp.zeros_like(joint)
        joint[0:levels, :] = lev_ref[...].astype(F32)
        joint[levels : levels + surf, :] = surf_ref[...].astype(F32)
        for pair in range(blocks.shape[0] // 2):
            both = joint[:, pair * 128 : pair * 128 + 128].astype(BF16)
            blocks[2 * pair] = both[:, :64]
            blocks[2 * pair + 1] = both[:, 64:]

    even[...] = jnp.zeros_like(even)
    odd[...] = jnp.zeros_like(odd)
    for pair in range(slots // 2):
        a, b = 2 * pair, 2 * pair + 1
        lhs = jnp.concatenate([blocks[src[0, o, a]], blocks[src[0, o, b]]], axis=0)
        got = dot(lhs, w_ref[0, 0, :, pair * 128 : pair * 128 + 128]).astype(BF16).astype(F32)
        to_a, to_b = dst[0, o, a], dst[0, o, b]
        to_a = jnp.where(to_a < 0, count, to_a)
        to_b = jnp.where(to_b < 0, count, to_b)
        even[to_a] = even[to_a] + got[:ROWS]
        odd[to_b] = odd[to_b] + got[32 : 32 + ROWS]
    low = lax.broadcasted_iota(jnp.int32, (ROWS, 128), 1) < 64

    def joined(t):
        left = even[2 * t] + pltpu.roll(odd[2 * t], 64, 1)
        right = pltpu.roll(even[2 * t + 1], 64, 1) + odd[2 * t + 1]
        return jnp.where(low, left, right)

    for t in range(0, count // 2, 2):
        both = jnp.concatenate([joined(t), joined(t + 1)], axis=0)
        out_ref[0, t * ROWS : (t + 2) * ROWS, :] = both.astype(BF16)


def middle_kernel(
    grp_n, dom_n, lev_n,
    agg, ice_cover, ice_flux, ocean_state, drag, level_weights, named,
    surf_out, lev_out, flux_out,
    sib, comb, recv, own, halo, counts, around, ice8, state8, lw_rows, surf8, flat, flux_send, flux_recv, col_send, col_recv,
    sib_s, sib_r, far_s, far_r, halo_s, halo_r, col_s, col_r, flux_s, flux_r,
):
    grp, dom, lev = lax.axis_index("grp"), lax.axis_index("dom"), lax.axis_index("lev")
    parts = grp_n * dom_n
    p = grp * dom_n + dom
    core = lax.rem(dom, 2)
    levels, surf = lev_out.shape[0], surf_out.shape[0]
    cells = lev_out.shape[1]
    tiles = cells // 128
    near = agg.shape[0]

    def part(by):
        q = lax.rem(p + by + parts, parts)
        return (q // dom_n, lax.rem(q, dom_n), lev)

    def ring(by):
        return (grp, lax.rem(dom + by + dom_n, dom_n), lev)

    def column_peer(by):
        return (grp, dom, lax.rem(lev + by, lev_n))

    sibling = (grp, dom + 1 - 2 * core, lev)

    barrier = pltpu.get_barrier_semaphore()
    greeted = 0
    for by in range(1, near + 1):
        for sign in (1, -1):
            pl.semaphore_signal(barrier, inc=1, device_id=part(sign * by), device_id_type=MESH)
            greeted += 1
    for by in (1, -1):
        pl.semaphore_signal(barrier, inc=1, device_id=ring(by), device_id_type=MESH)
        greeted += 1
    for by in range(1, lev_n):
        pl.semaphore_signal(barrier, inc=1, device_id=column_peer(by), device_id_type=MESH)
        greeted += 1
    pl.semaphore_wait(barrier, greeted)

    def copy(src, dst, send, got, device):
        return pltpu.make_async_remote_copy(
            src_ref=src, dst_ref=dst, send_sem=send, recv_sem=got, device_id=device, device_id_type=MESH
        )

    half = near // 2
    sib_copies = [copy(agg.at[2 * m + 1], sib.at[m], sib_s.at[m], sib_r.at[m], sibling) for m in range(half)]
    far_copies = [copy(comb.at[d - 1], recv.at[d - 1], far_s.at[d - 1], far_r.at[d - 1], part(2 * d)) for d in range(1, half)]
    last_copy = copy(sib.at[half - 1], recv.at[half - 1], far_s.at[half - 1], far_r.at[half - 1], part(2 * half))
    for m in reversed(range(half)):
        sib_copies[m].start()

    sib_copies[half - 1].wait_recv()

    @pl.when(core == 0)
    def _():
        last_copy.start()

    for d in reversed(range(1, half)):
        sib_copies[d - 1].wait_recv()
        comb[d - 1] = (agg[2 * d].astype(F32) + sib[d - 1 + core].astype(F32)).astype(BF16)
        far_copies[d - 1].start()

    def count_rows(i, carry):
        row = lax.broadcasted_iota(jnp.int32, (16, cells), 0) + i * 16
        total = jnp.zeros((16, cells), F32)
        for e in range(named.shape[0]):
            total = total + jnp.where(named[e : e + 1, :] == row, 1.0, 0.0)
        counts[pl.ds(pl.multiple_of(i * 16, 16), 16), :] = total.astype(BF16)
        return carry

    lax.fori_loop(0, counts.shape[0] // 16, count_rows, 0)

    first = levels - 16
    ice8[...] = jnp.zeros_like(ice8)
    state8[...] = jnp.zeros_like(state8)
    ice8[first : first + surf, :] = ice_flux[...].astype(F32)
    state8[first : first + surf, :] = ocean_state[...].astype(F32)
    lw_rows[...] = jnp.zeros_like(lw_rows)
    for k in range(levels):
        lw_rows[k : k + 1, :] = jnp.full((1, 128), level_weights[k], F32)

    for d in range(1, half):
        far_copies[d - 1].wait_recv()

    @pl.when(core == 0)
    def _():
        last_copy.wait_recv()

    @pl.when(core == 1)
    def _():
        recv[half - 1] = sib[0]

    is_surf = lax.broadcasted_iota(jnp.int32, (8, 128), 0) >= first
    for t in range(0, tiles, 2):
        rows = slice(t * ROWS, (t + 2) * ROWS)
        total = agg[0, rows, :].astype(F32)
        for d in range(half):
            total = total + recv[d, rows, :].astype(F32)
        for u in range(2):
            lanes = slice((t + u) * 128, (t + u + 1) * 128)
            one = total[u * ROWS : (u + 1) * ROWS]
            share = ice_cover[:, lanes]
            tail = jnp.where(is_surf, (1.0 - share) * one[16:] + share * ice8[:, lanes], one[16:])
            own[:, lanes] = jnp.concatenate([one[:16], tail, jnp.zeros((8, 128), F32)], axis=0).astype(BF16)

    to_prev = copy(own.at[:, 0:HW], halo.at[:, 0:HW], halo_s.at[0], halo_r.at[0], ring(-1))
    to_next = copy(own.at[:, cells - HW : cells], halo.at[:, HW : 2 * HW], halo_s.at[1], halo_r.at[1], ring(1))
    to_prev.start()
    to_next.start()
    for c in range(cells // 256):
        lanes = slice(c * 256, c * 256 + 256)
        around[:, lanes] = dot(own[...], counts[0:cells, lanes])
    to_prev.wait_recv()
    to_next.wait_recv()
    for c in range(cells // 256):
        lanes = slice(c * 256, c * 256 + 256)
        total = around[:, lanes] + dot(halo[...], counts[cells : cells + 2 * HW, lanes])
        forcing = (1.0 - KAPPA) * own[:, lanes].astype(F32) + (KAPPA / named.shape[0]) * total
        forcing = forcing[:ROWS]
        lev_out[:, lanes] = forcing[:levels]
        surf_out[:, lanes] = forcing[levels : levels + surf]
        surf8[:, lanes] = forcing[16:]
        weight = jnp.concatenate([lw_rows[...], lw_rows[...]], axis=1)
        col_send[:, lanes] = jnp.sum(weight * forcing, axis=0, keepdims=True)

    col_copies = [copy(col_send, col_recv.at[by - 1], col_s.at[by - 1], col_r.at[by - 1], column_peer(by)) for by in range(1, lev_n)]
    for one in col_copies:
        one.start()
    for one in col_copies:
        one.wait_recv()
    column = col_send[...]
    for by in range(1, lev_n):
        column = column + col_recv[by - 1]
    flux = drag[...] * (state8[...] - surf8[...] + column)
    for t in range(tiles):
        flat[t * surf : (t + 1) * surf, :] = flux[first : first + surf, t * 128 : t * 128 + 128]
    flux_send[...] = flat[...].astype(BF16)
    flux_copies = [copy(flux_send, flux_recv.at[o - 1], flux_s.at[o - 1], flux_r.at[o - 1], part(-o)) for o in range(1, near)]
    for one in reversed(flux_copies):
        one.start()
    flux_out[0] = flux_send[...]
    for o in range(1, near):
        flux_copies[o - 1].wait_recv()
        flux_out[o] = flux_recv[o - 1]

    for one in sib_copies + far_copies + [to_prev, to_next] + col_copies + flux_copies:
        one.wait_send()

    @pl.when(core == 0)
    def _():
        last_copy.wait_send()


def back_kernel(src, dst, flux_ref, w_ref, out_ref, flat, even, odd, total):
    o = pl.program_id(0)
    surf = out_ref.shape[0]
    width = w_ref.shape[2]
    slots = w_ref.shape[3] // width
    count = even.shape[0] - 1

    @pl.when(o == 0)
    def _():
        total[...] = jnp.zeros_like(total)
        even[...] = jnp.zeros_like(even)
        odd[...] = jnp.zeros_like(odd)

    flat[...] = flux_ref[0].astype(F32)
    low = lax.broadcasted_iota(jnp.int32, (surf, 128), 1) < 64
    zero = jnp.zeros((surf, 128), F32)
    for t in range(count // 2):
        here = flat[t * surf : (t + 1) * surf, :]
        there = pltpu.roll(here, 64, 1)
        even[2 * t, 0:surf, :] = jnp.where(low, here, zero)
        odd[2 * t, 0:surf, :] = jnp.where(low, zero, there)
        even[2 * t + 1, 0:surf, :] = jnp.where(low, there, zero)
        odd[2 * t + 1, 0:surf, :] = jnp.where(low, zero, here)
    for pair in range(slots // 2):
        a, b = 2 * pair, 2 * pair + 1
        to_a, to_b = dst[0, o, a], dst[0, o, b]
        to_a = jnp.where(to_a < 0, count, to_a)
        to_b = jnp.where(to_b < 0, count, to_b)
        lhs = jnp.concatenate([even[to_a], odd[to_b]], axis=0).astype(BF16)
        got = lax.dot_general(
            lhs, w_ref[0, 0, :, pair * 128 : pair * 128 + 128], (((1,), (1,)), ((), ())), preferred_element_type=F32
        )
        from_a, from_b = src[0, o, a], src[0, o, b]
        total[from_a] = total[from_a] + got[:8]
        total[from_b] = total[from_b] + got[8:]

    @pl.when(o == pl.num_programs(0) - 1)
    def _():
        for pair in range(total.shape[0] // 2):
            both = jnp.concatenate([total[2 * pair], total[2 * pair + 1]], axis=1)
            out_ref[:, pair * 128 : pair * 128 + 128] = both[:surf]


def shards(
    grp_n, dom_n, lev_n,
    atm_surface, atm_levels, margin_weights, src_block, dst_block, ice_cover, ice_flux, ocean_state, drag, level_weights,
    neighbours,
):
    surf, columns = atm_surface.shape
    levels = atm_levels.shape[0]
    near, width, across = margin_weights.shape[1:]
    cells = ice_cover.shape[0]
    tiles = cells // 128
    flat_rows = tiles * ROWS
    whole = lambda shape: pl.BlockSpec(shape, lambda o, *_: (0,) * len(shape))
    weights = pl.BlockSpec((1, 1, width, across), lambda o, *_: (0, o, 0, 0))
    agg = pl.pallas_call(
        forward_kernel,
        out_shape=jax.ShapeDtypeStruct((near, flat_rows, 128), BF16),
        grid_spec=pltpu.PrefetchScalarGridSpec(
            num_scalar_prefetch=2,
            grid=(near,),
            in_specs=[whole((surf, columns)), whole((levels, columns)), weights],
            out_specs=pl.BlockSpec((1, flat_rows, 128), lambda o, *_: (o, 0, 0)),
            scratch_shapes=[
                pltpu.VMEM((32, columns), F32),
                pltpu.VMEM((columns // width, 32, width), BF16),
                pltpu.VMEM((cells // width + 1, ROWS, 128), F32),
                pltpu.VMEM((cells // width + 1, ROWS, 128), F32),
            ],
        ),
        compiler_params=pltpu.CompilerParams(dimension_semantics=("arbitrary",), vmem_limit_bytes=32 * 2**20),
        name="pieces",
    )(src_block, dst_block, atm_surface, atm_levels, margin_weights)

    named = neighbours.T - HW
    named = jnp.where(named < 0, named + cells + 2 * HW, named)
    vmem = pl.BlockSpec(memory_space=pltpu.VMEM)
    dma = pltpu.SemaphoreType.DMA
    half = near // 2
    ocean_surface, ocean_levels, fluxes = pl.pallas_call(
        functools.partial(middle_kernel, grp_n, dom_n, lev_n),
        out_shape=[
            jax.ShapeDtypeStruct((surf, cells), F32),
            jax.ShapeDtypeStruct((levels, cells), F32),
            jax.ShapeDtypeStruct((near, tiles * surf, 128), BF16),
        ],
        in_specs=[vmem] * 5 + [pl.BlockSpec(memory_space=pltpu.SMEM), vmem],
        out_specs=[vmem] * 3,
        scratch_shapes=[
            pltpu.VMEM((half, flat_rows, 128), BF16),
            pltpu.VMEM((half - 1, flat_rows, 128), BF16),
            pltpu.VMEM((half, flat_rows, 128), BF16),
            pltpu.VMEM((32, cells), BF16),
            pltpu.VMEM((32, 2 * HW), BF16),
            pltpu.VMEM((cells + 2 * HW, cells), BF16),
            pltpu.VMEM((32, cells), F32),
            pltpu.VMEM((8, cells), F32),
            pltpu.VMEM((8, cells), F32),
            pltpu.VMEM((ROWS, 128), F32),
            pltpu.VMEM((8, cells), F32),
            pltpu.VMEM((tiles * surf, 128), F32),
            pltpu.VMEM((tiles * surf, 128), BF16),
            pltpu.VMEM((near - 1, tiles * surf, 128), BF16),
            pltpu.VMEM((1, cells), F32),
            pltpu.VMEM((max(lev_n - 1, 1), 1, cells), F32),
            dma((half,)), dma((half,)),
            dma((half,)), dma((half,)),
            dma((2,)), dma((2,)),
            dma((3,)), dma((3,)),
            dma((near - 1,)), dma((near - 1,)),
        ],
        compiler_params=pltpu.CompilerParams(collective_id=0, has_side_effects=True, vmem_limit_bytes=48 * 2**20),
        name="middle",
    )(agg, ice_cover.reshape(1, cells), ice_flux, ocean_state, drag.reshape(1, cells), level_weights, named)

    atm_flux = pl.pallas_call(
        back_kernel,
        out_shape=jax.ShapeDtypeStruct((surf, columns), F32),
        grid_spec=pltpu.PrefetchScalarGridSpec(
            num_scalar_prefetch=2,
            grid=(near,),
            in_specs=[pl.BlockSpec((1, tiles * surf, 128), lambda o, *_: (o, 0, 0)), weights],
            out_specs=whole((surf, columns)),
            scratch_shapes=[
                pltpu.VMEM((tiles * surf, 128), F32),
                pltpu.VMEM((cells // width + 1, 8, 128), F32),
                pltpu.VMEM((cells // width + 1, 8, 128), F32),
                pltpu.VMEM((columns // width, 8, width), F32),
            ],
        ),
        compiler_params=pltpu.CompilerParams(dimension_semantics=("arbitrary",), vmem_limit_bytes=32 * 2**20),
        name="back",
    )(src_block, dst_block, fluxes, margin_weights)
    return ocean_surface, ocean_levels, atm_flux


def solution(mesh):
    return jax.shard_map(
        functools.partial(shards, mesh.shape["grp"], mesh.shape["dom"], mesh.shape["lev"]),
        mesh=mesh,
        in_specs=(
            P("lev", ("grp", "dom")),
            P("lev", ("grp", "dom")),
            P(("grp", "dom"), None, None, None),
            P(("grp", "dom"), None, None),
            P(("grp", "dom"), None, None),
            P(("grp", "dom")),
            P("lev", ("grp", "dom")),
            P("lev", ("grp", "dom")),
            P(("grp", "dom")),
            P("lev"),
            P(("grp", "dom"), None),
        ),
        out_specs=(P("lev", ("grp", "dom")), P("lev", ("grp", "dom")), P("lev", ("grp", "dom"))),
        check_vma=False,
    )
```

time: 222 us -> 71.9 us (0.32)
  starting transfers between devices: 93.4 us -> 0 us
  local copies, waits for them, and re-layouts: 72.5 us -> 5.97 us
  Pallas kernels: 0 us -> 63.8 us
  waiting for transfers between devices: 19.7 us -> 0 us
  other arithmetic: 15.2 us -> 0.89 us
  matrix products: 9.66 us -> 0 us
  blocking collectives: 8.6 us -> 0 us
    ppermute x23 -> x0, starting transfers between devices: 93.4 us -> none  [the longest x21 92.9 us: from_behind(): lax.ppermute(x, axis, [(i, (i + by) % devices) for i in range(devices)])]
    pallas_call x0 -> x3, Pallas kernels: none -> 63.8 us  [the longest x1 55.2 us: shards(): pl.pallas_call(functools.partial(middle_kernel, grp_n, dom_n, lev_n), out...]
    gather x3 -> x0, local copies, waits for them, and re-layouts: 51.3 us -> none  [the longest x2 50.3 us: shards(): jnp.take(extended, neighbours.reshape(-1), axis=1)]
    ppermute x23 -> x0, waiting for transfers between devices: 19.7 us -> none  [the longest x21 17 us: from_behind(): lax.ppermute(x, axis, [(i, (i + by) % devices) for i in range(devices)])]
    reduce_sum x2 -> x0, other arithmetic: 13.5 us -> none  [the longest x1 12.8 us: shards(): jnp.sum(nearby.astype(jnp.float32), axis=2) / neighbours.shape[1]]
    another operation x12 -> x0, local copies, waits for them, and re-layouts: 12 us -> none  [the longest x1 7.1 us: shards(): weight_mat = margin_weights[0].reshape(near, width, slots, width)]
    dot_general x5 -> x0, matrix products: 9.66 us -> none  [the longest x1 4.47 us: shards(): jnp.einsum('ocsj,oicj->ocsi', returned, weight_mat, preferred_element_typ...]
    psum x1 -> x0, blocking collectives: 8.6 us -> none  [shards(): lax.psum(jnp.sum(level_weights[:, None] * forcing[surf_dev:], axis=0), 'l...]
  transfers between devices with their start and end apart: 23 -> 0, of which waited for: 7 -> 0; matrix products, arithmetic and copies ran while one was open for 4% -> 0% of each run, Pallas kernels for 0% -> 0%
where the time goes in v1:
time: 71.9 us; the launch traced here: 71.5 us
  Pallas kernels  63.8 us (89%)
  local copies, waits for them, and re-layouts  5.97 us (8%)
  other arithmetic  0.89 us (1%)
  between operations  0.78 us (1%)
    pallas_call x1, Pallas kernels, shards(): pl.pallas_call(functools.partial(middle_kernel, grp_n, dom_n, lev_n), out...  55.2 us
    unnamed x28, local copies, waits for them, and re-layouts  5.97 us
    pallas_call x1, Pallas kernels, shards(): pl.pallas_call(forward_kernel, out_shape=jax.ShapeDtypeStruct((near, flat...  4.34 us
    pallas_call x1, Pallas kernels, shards(): pl.pallas_call(back_kernel, out_shape=jax.ShapeDtypeStruct((surf, columns...  4.3 us

profile of v1, /device:TPU:1, one launch (start us, length us, event | category | flops | bytes accessed | tf_op | source)
XLA Modules:
  0.0 71.5 jit_solution(18303153327696935285)
XLA Ops:
  0.6 0.0 copy-start.9
  0.6 0.0 copy-start.7
  0.7 0.0 copy-start.12
  0.7 0.0 copy-start.11
  0.7 0.0 copy-start.5
  0.7 0.0 copy-start.4
  0.7 0.0 copy-start.10
  0.7 0.9 %compare_select_fusion.named = s32[6,2048]{1,0:T(8,128)S(1)} fusion(s32[2048,6]{0,1:T(8,128)} %param.21), kind=kLoop, calls=%fused_computation | loop fusion | flops 49152 | bytes 98304 | tf_op jit(solution)/shard_map/jit(_where)/select_n | solution.py:294
  1.6 0.0 copy-start
  1.6 1.6 %copy-done = bf16[1,8,64,2048]{3,2,1,0:T(8,128)(2,1)S(1)} copy-done((bf16[1,8,64,2048]{3,2,1,0:T(8,128)(2,1)S(1)}, bf16[1,8,64,2048]{3,2,1,0:T(8,128)(2,1)}, u32[]{:S(2)}) %copy-start) | copy-done | bytes 2097176
  3.2 0.9 %copy-done.2 = bf16[20,4096]{1,0:T(8,128)(2,1)S(1)} copy-done((bf16[20,4096]{1,0:T(8,128)(2,1)S(1)}, bf16[20,4096]{1,0:T(8,128)(2,1)}, u32[]{:S(2)}) %copy-start.2) | copy-done | bytes 163864
  4.1 0.8 %copy-done.3 = bf16[3,4096]{1,0:T(4,128)(2,1)S(1)} copy-done((bf16[3,4096]{1,0:T(4,128)(2,1)S(1)}, bf16[3,4096]{1,0:T(4,128)(2,1)}, u32[]{:S(2)}) %copy-start.3) | copy-done | bytes 24600
  4.9 0.7 copy-done.6
  5.6 0.7 copy-done.8
  6.3 4.3 %pieces.1.agg = bf16[8,384,128]{2,1,0:T(8,128)(2,1)S(1)} custom-call(s32[1,8,32]{2,1,0:T(8,128)S(1)} %copy-done.6, s32[1,8,32]{2,1,0:T(8,128)S(1)} %copy-done.8, bf16[3,4096]{1,0:T(4,128)(2,1)S(1)} %copy-done.3, bf16[20,4096]{1,0:T(8,128)(2,1)S(1)} %copy-done.2, bf16[1,8,64,2048]{3,2,1,0:T(8,128)(2,1)S(1)} %copy-done), custom_call_target="tpu_custom_call" | custom-call | tf_op jit(solution)/shard_map/pieces/pallas_call | solution.py:274
  10.6 0.0 copy-done.12
  10.6 0.0 copy-done.11
  10.6 0.0 copy-done.5
  10.6 0.0 copy-done.4
  10.6 0.0 copy-done.10
  10.7 55.2 %middle.1 = (f32[3,2048]{1,0:T(4,128)S(1)}, f32[20,2048]{1,0:T(8,128)S(1)}, bf16[8,48,128]{2,1,0:T(8,128)(2,1)S(1)}) custom-call(bf16[8,384,128]{2,1,0:T(8,128)(2,1)S(1)} %pieces.1.agg, f32[1,2048]{1,0:T(1,128)S(1)} %bitcast.6, bf16[3,2048]{1,0:T(4,128)(2,1)S(1)} %copy-done.4, bf16[3,2048]{1,0:T(4,128)(2,1)S(1)} %copy-done.5, f32[1,2048]{1,0:T(1,128)S(1)} %bitcast.7, ...), custom_call_target="tpu_custom_call" | custom-call | tf_op jit(solution)/shard_map/middle/pallas_call | solution.py:298
  65.9 4.3 %back.1 = f32[3,4096]{1,0:T(4,128)} custom-call(s32[1,8,32]{2,1,0:T(8,128)S(1)} %copy-done.7, s32[1,8,32]{2,1,0:T(8,128)S(1)} %copy-done.9, bf16[8,48,128]{2,1,0:T(8,128)(2,1)S(1)} %get-tuple-element.8.flux_ref, bf16[1,8,64,2048]{3,2,1,0:T(8,128)(2,1)S(1)} %copy-done.1), custom_call_target="tpu_custom_call" | custom-call | tf_op jit(solution)/shard_map/back/pallas_call | solution.py:334
  70.2 0.6 copy.16
  70.8 0.7 copy.17
  (8 shorter events, 0.0 us)
Async XLA Ops:
  0.6 65.2 %copy-start.9 = (s32[1,8,32]{2,1,0:T(8,128)S(1)}, s32[1,8,32]{2,1,0:T(8,128)}, u32[]{:S(2)}) copy-start(s32[1,8,32]{2,1,0:T(8,128)} %dst.3) | copy-start | bytes 3076
  0.6 65.2 %copy-start.7 = (s32[1,8,32]{2,1,0:T(8,128)S(1)}, s32[1,8,32]{2,1,0:T(8,128)}, u32[]{:S(2)}) copy-start(s32[1,8,32]{2,1,0:T(8,128)} %src.3) | copy-start | bytes 3076
  0.7 10.0 %copy-start.12 = (f32[20]{0:T(128)S(1)}, f32[20]{0:T(128)}, u32[]{:S(2)}) copy-start(f32[20]{0:T(128)} %level_weights.1) | copy-start | bytes 244
  0.7 10.0 %copy-start.11 = (f32[2048]{0:T(1024)S(1)}, f32[2048]{0:T(1024)}, u32[]{:S(2)}) copy-start(f32[2048]{0:T(1024)} %param.19) | copy-start | bytes 24580
  0.7 10.0 %copy-start.5 = (bf16[3,2048]{1,0:T(4,128)(2,1)S(1)}, bf16[3,2048]{1,0:T(4,128)(2,1)}, u32[]{:S(2)}) copy-start(bf16[3,2048]{1,0:T(4,128)(2,1)} %ocean_state.1) | copy-start | bytes 36868
  0.7 10.0 %copy-start.4 = (bf16[3,2048]{1,0:T(4,128)(2,1)S(1)}, bf16[3,2048]{1,0:T(4,128)(2,1)}, u32[]{:S(2)}) copy-start(bf16[3,2048]{1,0:T(4,128)(2,1)} %ice_flux.1) | copy-start | bytes 36868
  0.7 10.0 %copy-start.10 = (f32[2048]{0:T(1024)S(1)}, f32[2048]{0:T(1024)}, u32[]{:S(2)}) copy-start(f32[2048]{0:T(1024)} %param.16) | copy-start | bytes 24580
  1.6 1.6 %copy-start = (bf16[1,8,64,2048]{3,2,1,0:T(8,128)(2,1)S(1)}, bf16[1,8,64,2048]{3,2,1,0:T(8,128)(2,1)}, u32[]{:S(2)}) copy-start(bf16[1,8,64,2048]{3,2,1,0:T(8,128)(2,1)} %w_ref.3) | copy-start | bytes 6291460
  3.2 0.9 %copy-start.2 = (bf16[20,4096]{1,0:T(8,128)(2,1)S(1)}, bf16[20,4096]{1,0:T(8,128)(2,1)}, u32[]{:S(2)}) copy-start(bf16[20,4096]{1,0:T(8,128)(2,1)} %lev_ref.1) | copy-start | bytes 491524
  4.1 0.8 %copy-start.3 = (bf16[3,4096]{1,0:T(4,128)(2,1)S(1)}, bf16[3,4096]{1,0:T(4,128)(2,1)}, u32[]{:S(2)}) copy-start(bf16[3,4096]{1,0:T(4,128)(2,1)} %surf_ref.1) | copy-start | bytes 73732
  4.9 0.7 copy-start.6
  5.6 0.7 copy-start.8
  6.3 59.6 %copy-start.1 = (bf16[1,8,64,2048]{3,2,1,0:T(8,128)(2,1)S(1)}, bf16[1,8,64,2048]{3,2,1,0:T(8,128)(2,1)}, u32[]{:S(2)}) copy-start(bf16[1,8,64,2048]{3,2,1,0:T(8,128)(2,1)} %w_ref.3) | copy-start | bytes 6291460

commit v2 on v1

v2 whole, which is shorter than its diff:
```python
import functools

import jax
import jax.numpy as jnp
from jax import lax
from jax.experimental import pallas as pl
from jax.experimental.pallas import tpu as pltpu
from jax.sharding import PartitionSpec as P

HW = 128
KAPPA = 0.5
ROWS = 24
MESH = pl.DeviceIdType.MESH
F32 = jnp.float32
BF16 = jnp.bfloat16


def dot(a, b):
    return jnp.dot(a, b, preferred_element_type=F32)


def forward_kernel(src_hbm, dst_hbm, surf_hbm, lev_hbm, w_hbm, out_ref, src, dst, surf_ref, lev_ref, w_ref, joint, blocks, even, odd, small, big):
    levels, surf = lev_ref.shape[0], surf_ref.shape[0]
    near, width, across = w_ref.shape
    slots = across // width
    count = even.shape[0] - 1
    arriving = [
        pltpu.make_async_copy(here, there, small.at[n])
        for n, (here, there) in enumerate([(lev_hbm, lev_ref), (surf_hbm, surf_ref), (src_hbm.at[0], src), (dst_hbm.at[0], dst)])
    ]
    weights = [pltpu.make_async_copy(w_hbm.at[0, o], w_ref.at[o], big.at[o]) for o in range(near)]
    for one in arriving + weights:
        one.start()
    joint[levels + surf :, :] = jnp.zeros_like(joint[levels + surf :, :])
    arriving[0].wait()
    arriving[1].wait()
    joint[0:levels, :] = lev_ref[...].astype(F32)
    joint[levels : levels + surf, :] = surf_ref[...].astype(F32)
    for pair in range(blocks.shape[0] // 2):
        both = joint[:, pair * 128 : pair * 128 + 128].astype(BF16)
        blocks[2 * pair] = both[:, :64]
        blocks[2 * pair + 1] = both[:, 64:]
    arriving[2].wait()
    arriving[3].wait()
    low = lax.broadcasted_iota(jnp.int32, (ROWS, 128), 1) < 64

    def offset(o, carry):
        pltpu.make_async_copy(w_hbm.at[0, o], w_ref.at[o], big.at[o]).wait()
        even[...] = jnp.zeros_like(even)
        odd[...] = jnp.zeros_like(odd)
        for pair in range(slots // 2):
            a, b = 2 * pair, 2 * pair + 1
            lhs = jnp.concatenate([blocks[src[o, a]], blocks[src[o, b]]], axis=0)
            got = dot(lhs, w_ref[o, :, pair * 128 : pair * 128 + 128]).astype(BF16).astype(F32)
            to_a, to_b = dst[o, a], dst[o, b]
            to_a = jnp.where(to_a < 0, count, to_a)
            to_b = jnp.where(to_b < 0, count, to_b)
            even[to_a] = even[to_a] + got[:ROWS]
            odd[to_b] = odd[to_b] + got[32 : 32 + ROWS]

        def joined(t):
            left = even[2 * t] + pltpu.roll(odd[2 * t], 64, 1)
            right = pltpu.roll(even[2 * t + 1], 64, 1) + odd[2 * t + 1]
            return jnp.where(low, left, right)

        for t in range(0, count // 2, 2):
            both = jnp.concatenate([joined(t), joined(t + 1)], axis=0)
            out_ref[o, t * ROWS : (t + 2) * ROWS, :] = both.astype(BF16)
        return carry

    lax.fori_loop(0, near, offset, 0)


def middle_kernel(
    grp_n, dom_n, lev_n,
    agg, ice_cover, ice_flux, ocean_state, drag, level_weights, neighbours,
    surf_out, lev_out, flux_out,
    sib, comb, recv, own, halo, named, hits, counts, around, ice8, state8, lw_rows, surf8, flat, flux_send, flux_recv, col_send, col_recv,
    sib_s, sib_r, far_s, far_r, halo_s, halo_r, col_s, col_r, flux_s, flux_r,
):
    grp, dom, lev = lax.axis_index("grp"), lax.axis_index("dom"), lax.axis_index("lev")
    parts = grp_n * dom_n
    p = grp * dom_n + dom
    core = lax.rem(dom, 2)
    levels, surf = lev_out.shape[0], surf_out.shape[0]
    cells = lev_out.shape[1]
    tiles = cells // 128
    near = agg.shape[0]

    def part(by):
        q = lax.rem(p + by + parts, parts)
        return (q // dom_n, lax.rem(q, dom_n), lev)

    def ring(by):
        return (grp, lax.rem(dom + by + dom_n, dom_n), lev)

    def column_peer(by):
        return (grp, dom, lax.rem(lev + by, lev_n))

    sibling = (grp, dom + 1 - 2 * core, lev)

    barrier = pltpu.get_barrier_semaphore()
    greeted = 0
    for by in range(1, near + 1):
        for sign in (1, -1):
            pl.semaphore_signal(barrier, inc=1, device_id=part(sign * by), device_id_type=MESH)
            greeted += 1
    for by in (1, -1):
        pl.semaphore_signal(barrier, inc=1, device_id=ring(by), device_id_type=MESH)
        greeted += 1
    for by in range(1, lev_n):
        pl.semaphore_signal(barrier, inc=1, device_id=column_peer(by), device_id_type=MESH)
        greeted += 1
    pl.semaphore_wait(barrier, greeted)

    def copy(src, dst, send, got, device):
        return pltpu.make_async_remote_copy(
            src_ref=src, dst_ref=dst, send_sem=send, recv_sem=got, device_id=device, device_id_type=MESH
        )

    sib_copies = [copy(agg.at[2 * m + 1], sib.at[m], sib_s.at[m], sib_r.at[m], sibling) for m in range(3)]
    sib_copies.append(copy(agg.at[7], sib.at[3], sib_s.at[3], sib_r.at[3], part(1)))
    far1 = copy(comb.at[0], recv.at[0], far_s.at[0], far_r.at[0], part(2))
    far2 = copy(comb.at[1], recv.at[1], far_s.at[1], far_r.at[1], part(4))
    far3 = copy(comb.at[2], recv.at[2], far_s.at[2], far_r.at[2], part(2))
    for m in reversed(range(4)):
        sib_copies[m].start()

    def wide(ref, n):
        return ref[n].astype(F32)

    sib_copies[3].wait_recv()
    sib_copies[2].wait_recv()
    comb[2] = (wide(agg, 6) + wide(sib, 3) + jnp.where(core == 0, wide(sib, 2), 0.0)).astype(BF16)
    far3.start()
    sib_copies[1].wait_recv()
    sib_copies[0].wait_recv()
    comb[0] = (wide(agg, 2) + wide(sib, core)).astype(BF16)
    far1.start()

    nb = named.shape[0]
    ext_tiles = counts.shape[0] // 128
    place = neighbours[...] - HW
    named[...] = jnp.where(place < 0, place + cells + 2 * HW, place)

    def hit_rows(h, carry):
        for e in range(nb):
            hit = jnp.where(jnp.broadcast_to(named[e : e + 1, :] // 128, (16, cells)) == h, 1.0, 0.0)
            hits[e, pl.ds(pl.multiple_of(h * 16, 16), 16), :] = hit.astype(BF16)
        return carry

    def count_cells(n, carry):
        lanes = pl.ds(pl.multiple_of(n * 128, 128), 128)
        rows = [jnp.broadcast_to(named[e : e + 1, lanes] % 128, (16, 128)) for e in range(nb)]

        def block(lb, carry):
            row = lax.broadcasted_iota(jnp.int32, (16, 128), 0) + lb * 16
            spots = [jnp.where(rows[e] == row, 1.0, 0.0).astype(BF16) for e in range(nb)]
            for h in range(ext_tiles):
                total = spots[0] * hits[0, h * 16 : h * 16 + 16, lanes]
                for e in range(1, nb):
                    total = total + spots[e] * hits[e, h * 16 : h * 16 + 16, lanes]
                counts[pl.ds(pl.multiple_of(h * 128 + lb * 16, 16), 16), lanes] = total
            return carry

        return lax.fori_loop(0, 8, block, carry)

    lax.fori_loop(0, ext_tiles, hit_rows, 0)
    far3.wait_recv()
    comb[1] = (wide(agg, 4) + wide(sib, 1 + core) + wide(recv, 2)).astype(BF16)
    far2.start()
    lax.fori_loop(0, tiles, count_cells, 0)

    first = levels - 16
    ice8[...] = jnp.zeros_like(ice8)
    state8[...] = jnp.zeros_like(state8)
    ice8[first : first + surf, :] = ice_flux[...].astype(F32)
    state8[first : first + surf, :] = ocean_state[...].astype(F32)
    lw_rows[...] = jnp.zeros_like(lw_rows)
    for k in range(levels):
        lw_rows[k : k + 1, :] = jnp.full((1, 128), level_weights[k], F32)

    far1.wait_recv()
    far2.wait_recv()

    is_surf = lax.broadcasted_iota(jnp.int32, (8, 128), 0) >= first
    for t in range(0, tiles, 2):
        rows = slice(t * ROWS, (t + 2) * ROWS)
        total = agg[0, rows, :].astype(F32) + recv[0, rows, :].astype(F32) + recv[1, rows, :].astype(F32)
        total = total + jnp.where(core == 1, sib[0, rows, :].astype(F32), 0.0)
        for u in range(2):
            lanes = slice((t + u) * 128, (t + u + 1) * 128)
            one = total[u * ROWS : (u + 1) * ROWS]
            share = ice_cover[:, lanes]
            tail = jnp.where(is_surf, (1.0 - share) * one[16:] + share * ice8[:, lanes], one[16:])
            own[:, lanes] = jnp.concatenate([one[:16], tail, jnp.zeros((8, 128), F32)], axis=0).astype(BF16)

    to_prev = copy(own.at[:, 0:HW], halo.at[:, 0:HW], halo_s.at[0], halo_r.at[0], ring(-1))
    to_next = copy(own.at[:, cells - HW : cells], halo.at[:, HW : 2 * HW], halo_s.at[1], halo_r.at[1], ring(1))
    to_prev.start()
    to_next.start()
    for c in range(cells // 256):
        lanes = slice(c * 256, c * 256 + 256)
        around[:, lanes] = dot(own[...], counts[0:cells, lanes])
    to_prev.wait_recv()
    to_next.wait_recv()
    for c in range(cells // 256):
        lanes = slice(c * 256, c * 256 + 256)
        total = around[:, lanes] + dot(halo[...], counts[cells : cells + 2 * HW, lanes])
        forcing = (1.0 - KAPPA) * own[:, lanes].astype(F32) + (KAPPA / named.shape[0]) * total
        forcing = forcing[:ROWS]
        lev_out[:, lanes] = forcing[:levels]
        surf_out[:, lanes] = forcing[levels : levels + surf]
        surf8[:, lanes] = forcing[16:]
        weight = jnp.concatenate([lw_rows[...], lw_rows[...]], axis=1)
        col_send[:, lanes] = jnp.sum(weight * forcing, axis=0, keepdims=True)

    col_copies = [copy(col_send, col_recv.at[by - 1], col_s.at[by - 1], col_r.at[by - 1], column_peer(by)) for by in range(1, lev_n)]
    for one in col_copies:
        one.start()
    for one in col_copies:
        one.wait_recv()
    column = col_send[...]
    for by in range(1, lev_n):
        column = column + col_recv[by - 1]
    flux = drag[...] * (state8[...] - surf8[...] + column)
    for t in range(tiles):
        flat[t * surf : (t + 1) * surf, :] = flux[first : first + surf, t * 128 : t * 128 + 128]
    flux_send[...] = flat[...].astype(BF16)
    flux_copies = [copy(flux_send, flux_recv.at[o - 1], flux_s.at[o - 1], flux_r.at[o - 1], part(-o)) for o in range(1, near)]
    for one in reversed(flux_copies):
        one.start()
    flux_out[0] = flux_send[...]
    for o in range(1, near):
        flux_copies[o - 1].wait_recv()
        flux_out[o] = flux_recv[o - 1]

    for one in sib_copies + [far1, far2, far3, to_prev, to_next] + col_copies + flux_copies:
        one.wait_send()


def back_kernel(src_hbm, dst_hbm, flux_ref, w_ref, surf_ref, lev_ref, out_ref, surf_out, lev_out, src, dst, flat, even, odd, total, sems):
    surf = out_ref.shape[0]
    near, width, across = w_ref.shape[1:]
    slots = across // width
    count = even.shape[0] // near - 1
    copies = [
        pltpu.make_async_copy(here, there, sems.at[n])
        for n, (here, there) in enumerate([(src_hbm.at[0], src), (dst_hbm.at[0], dst), (surf_ref, surf_out), (lev_ref, lev_out)])
    ]
    for one in copies:
        one.start()
    total[...] = jnp.zeros_like(total)
    even[...] = jnp.zeros_like(even)
    odd[...] = jnp.zeros_like(odd)
    low = lax.broadcasted_iota(jnp.int32, (surf, 128), 1) < 64
    zero = jnp.zeros((surf, 128), F32)
    flat[...] = flux_ref[...].astype(F32)

    def spread(o, carry):
        base = o * (count + 1)
        for t in range(count // 2):
            here = flat[o, t * surf : (t + 1) * surf, :]
            there = pltpu.roll(here, 64, 1)
            even[base + 2 * t, 0:surf, :] = jnp.where(low, here, zero)
            odd[base + 2 * t, 0:surf, :] = jnp.where(low, zero, there)
            even[base + 2 * t + 1, 0:surf, :] = jnp.where(low, there, zero)
            odd[base + 2 * t + 1, 0:surf, :] = jnp.where(low, zero, here)
        return carry

    lax.fori_loop(0, near, spread, 0)
    copies[0].wait()
    copies[1].wait()

    def offset(o, carry):
        base = o * (count + 1)
        for pair in range(slots // 2):
            a, b = 2 * pair, 2 * pair + 1
            to_a, to_b = dst[o, a], dst[o, b]
            to_a = jnp.where(to_a < 0, count, to_a)
            to_b = jnp.where(to_b < 0, count, to_b)
            lhs = jnp.concatenate([even[base + to_a], odd[base + to_b]], axis=0).astype(BF16)
            got = lax.dot_general(
                lhs, w_ref[0, o, :, pair * 128 : pair * 128 + 128], (((1,), (1,)), ((), ())), preferred_element_type=F32
            )
            from_a, from_b = src[o, a], src[o, b]
            total[from_a] = total[from_a] + got[:8]
            total[from_b] = total[from_b] + got[8:]
        return carry

    lax.fori_loop(0, near, offset, 0)
    for pair in range(total.shape[0] // 2):
        both = jnp.concatenate([total[2 * pair], total[2 * pair + 1]], axis=1)
        out_ref[:, pair * 128 : pair * 128 + 128] = both[:surf]
    copies[2].wait()
    copies[3].wait()


def shards(
    grp_n, dom_n, lev_n,
    atm_surface, atm_levels, margin_weights, src_block, dst_block, ice_cover, ice_flux, ocean_state, drag, level_weights,
    neighbours,
):
    surf, columns = atm_surface.shape
    levels = atm_levels.shape[0]
    near, width, across = margin_weights.shape[1:]
    cells = ice_cover.shape[0]
    tiles = cells // 128
    flat_rows = tiles * ROWS
    hbm = pl.BlockSpec(memory_space=pltpu.HBM)
    dma = pltpu.SemaphoreType.DMA
    agg = pl.pallas_call(
        forward_kernel,
        out_shape=jax.ShapeDtypeStruct((near, flat_rows, 128), BF16),
        in_specs=[hbm] * 5,
        out_specs=pl.BlockSpec(memory_space=pltpu.VMEM),
        scratch_shapes=[
            pltpu.SMEM(src_block.shape[1:], jnp.int32),
            pltpu.SMEM(src_block.shape[1:], jnp.int32),
            pltpu.VMEM((surf, columns), BF16),
            pltpu.VMEM((levels, columns), BF16),
            pltpu.VMEM((near, width, across), BF16),
            pltpu.VMEM((32, columns), F32),
            pltpu.VMEM((columns // width, 32, width), BF16),
            pltpu.VMEM((cells // width + 1, ROWS, 128), F32),
            pltpu.VMEM((cells // width + 1, ROWS, 128), F32),
            dma((4,)),
            dma((near,)),
        ],
        compiler_params=pltpu.CompilerParams(vmem_limit_bytes=32 * 2**20),
        name="pieces",
    )(*[pltpu.with_memory_space_constraint(x, pltpu.HBM) for x in (src_block, dst_block, atm_surface, atm_levels, margin_weights)])

    vmem = pl.BlockSpec(memory_space=pltpu.VMEM)
    ocean_surface, ocean_levels, fluxes = pl.pallas_call(
        functools.partial(middle_kernel, grp_n, dom_n, lev_n),
        out_shape=[
            jax.ShapeDtypeStruct((surf, cells), F32),
            jax.ShapeDtypeStruct((levels, cells), F32),
            jax.ShapeDtypeStruct((near, tiles * surf, 128), BF16),
        ],
        in_specs=[vmem] * 5 + [pl.BlockSpec(memory_space=pltpu.SMEM), vmem],
        out_specs=[vmem] * 3,
        scratch_shapes=[
            pltpu.VMEM((4, flat_rows, 128), BF16),
            pltpu.VMEM((3, flat_rows, 128), BF16),
            pltpu.VMEM((3, flat_rows, 128), BF16),
            pltpu.VMEM((32, cells), BF16),
            pltpu.VMEM((32, 2 * HW), BF16),
            pltpu.VMEM((neighbours.shape[1], cells), jnp.int32),
            pltpu.VMEM((neighbours.shape[1], (cells + 2 * HW) // 8, cells), BF16),
            pltpu.VMEM((cells + 2 * HW, cells), BF16),
            pltpu.VMEM((32, cells), F32),
            pltpu.VMEM((8, cells), F32),
            pltpu.VMEM((8, cells), F32),
            pltpu.VMEM((ROWS, 128), F32),
            pltpu.VMEM((8, cells), F32),
            pltpu.VMEM((tiles * surf, 128), F32),
            pltpu.VMEM((tiles * surf, 128), BF16),
            pltpu.VMEM((near - 1, tiles * surf, 128), BF16),
            pltpu.VMEM((1, cells), F32),
            pltpu.VMEM((max(lev_n - 1, 1), 1, cells), F32),
            dma((4,)), dma((4,)),
            dma((3,)), dma((3,)),
            dma((2,)), dma((2,)),
            dma((3,)), dma((3,)),
            dma((near - 1,)), dma((near - 1,)),
        ],
        compiler_params=pltpu.CompilerParams(collective_id=0, has_side_effects=True, vmem_limit_bytes=48 * 2**20),
        name="middle",
    )(agg, ice_cover.reshape(1, cells), ice_flux, ocean_state, drag.reshape(1, cells), level_weights, neighbours.T)

    atm_flux, ocean_surface, ocean_levels = pl.pallas_call(
        back_kernel,
        out_shape=[
            jax.ShapeDtypeStruct((surf, columns), F32),
            jax.ShapeDtypeStruct((surf, cells), F32),
            jax.ShapeDtypeStruct((levels, cells), F32),
        ],
        in_specs=[hbm] * 2 + [vmem] * 4,
        out_specs=[vmem, hbm, hbm],
        scratch_shapes=[
            pltpu.SMEM(src_block.shape[1:], jnp.int32),
            pltpu.SMEM(src_block.shape[1:], jnp.int32),
            pltpu.VMEM((near, tiles * surf, 128), F32),
            pltpu.VMEM((near * (cells // width + 1), 8, 128), F32),
            pltpu.VMEM((near * (cells // width + 1), 8, 128), F32),
            pltpu.VMEM((columns // width, 8, width), F32),
            dma((4,)),
        ],
        compiler_params=pltpu.CompilerParams(vmem_limit_bytes=32 * 2**20),
        name="back",
    )(src_block, dst_block, fluxes, margin_weights, ocean_surface, ocean_levels)
    return ocean_surface, ocean_levels, atm_flux


def solution(mesh):
    return jax.shard_map(
        functools.partial(shards, mesh.shape["grp"], mesh.shape["dom"], mesh.shape["lev"]),
        mesh=mesh,
        in_specs=(
            P("lev", ("grp", "dom")),
            P("lev", ("grp", "dom")),
            P(("grp", "dom"), None, None, None),
            P(("grp", "dom"), None, None),
            P(("grp", "dom"), None, None),
            P(("grp", "dom")),
            P("lev", ("grp", "dom")),
            P("lev", ("grp", "dom")),
            P(("grp", "dom")),
            P("lev"),
            P(("grp", "dom"), None),
        ),
        out_specs=(P("lev", ("grp", "dom")), P("lev", ("grp", "dom")), P("lev", ("grp", "dom"))),
        check_vma=False,
    )
```

time: 71.9 us -> 70.3 us (0.978)
  local copies, waits for them, and re-layouts: 5.97 us -> 0.04 us
  Pallas kernels: 63.8 us -> 69.3 us
  other arithmetic: 0.89 us -> 0 us
    unnamed x28 -> x18, local copies, waits for them, and re-layouts: 5.97 us -> 0.04 us
    pallas_call x1, Pallas kernels: 55.2 us -> 60.4 us  [shards(): pl.pallas_call(functools.partial(middle_kernel, grp_n, dom_n, lev_n), out...]
    select_n x1 -> x0, other arithmetic: 0.89 us -> none  [shards(): named = jnp.where(named < 0, named + cells + 2 * HW, named)]
    pallas_call x1, Pallas kernels: 4.34 us -> 5.09 us  [shards(): pl.pallas_call(forward_kernel, out_shape=jax.ShapeDtypeStruct((near, flat...]
where the time goes in v2:
time: 70.3 us; the launch traced here: 70.2 us
  Pallas kernels  69.3 us (99%)
  between operations  0.79 us (1%)
    pallas_call x1, Pallas kernels, shards(): pl.pallas_call(functools.partial(middle_kernel, grp_n, dom_n, lev_n), out...  60.4 us
    pallas_call x1, Pallas kernels, shards(): pl.pallas_call(forward_kernel, out_shape=jax.ShapeDtypeStruct((near, flat...  5.09 us
    pallas_call x1, Pallas kernels, shards(): pl.pallas_call(back_kernel, out_shape=[jax.ShapeDtypeStruct((surf, column...  3.83 us

profile of v2, /device:TPU:1, one launch (start us, length us, event | category | flops | bytes accessed | tf_op | source)
XLA Modules:
  0.0 70.2 jit_solution(14782699076451194721)
XLA Ops:
  0.6 0.0 copy-start.5
  0.6 0.0 copy-start.4
  0.7 0.0 copy-start
  0.7 0.0 copy-start.1
  0.7 0.0 copy-start.8
  0.7 0.0 copy-start.7
  0.7 0.0 copy-start.3
  0.7 0.0 copy-start.2
  0.7 0.0 copy-start.6
  0.7 5.1 %pieces.1.agg = bf16[8,384,128]{2,1,0:T(8,128)(2,1)S(1)} custom-call(s32[1,8,32]{2,1,0:T(8,128)} %src_hbm.3, s32[1,8,32]{2,1,0:T(8,128)} %dst_hbm.3, bf16[3,4096]{1,0:T(4,128)(2,1)} %surf_hbm.1, bf16[20,4096]{1,0:T(8,128)(2,1)} %lev_hbm.1, bf16[1,8,64,2048]{3,2,1,0:T(8,128)(2,1)} %w_ref.1), custom_call_target="tpu_custom_call" | custom-call | tf_op jit(solution)/shard_map/pieces/pallas_call | solution.py:312
  5.8 0.0 copy-done.1
  5.8 0.0 copy-done.8
  5.8 0.0 copy-done.7
  5.9 0.0 copy-done.3
  5.9 0.0 copy-done.2
  5.9 0.0 copy-done.6
  5.9 60.4 %middle.1 = (f32[3,2048]{1,0:T(4,128)S(1)}, f32[20,2048]{1,0:T(8,128)S(1)}, bf16[8,48,128]{2,1,0:T(8,128)(2,1)S(1)}) custom-call(bf16[8,384,128]{2,1,0:T(8,128)(2,1)S(1)} %pieces.1.agg, f32[1,2048]{1,0:T(1,128)S(1)} %bitcast.4, bf16[3,2048]{1,0:T(4,128)(2,1)S(1)} %copy-done.2, bf16[3,2048]{1,0:T(4,128)(2,1)S(1)} %copy-done.3, f32[1,2048]{1,0:T(1,128)S(1)} %bitcast.5, ...), custom_call_target="tpu_custom_call" | custom-call | tf_op jit(solution)/shard_map/middle/pallas_call | solution.py:335
  66.3 0.0 copy-done.5
  66.3 0.0 copy-done.4
  66.3 0.0 copy-done
  66.3 3.8 %back.1 = (f32[3,4096]{1,0:T(4,128)}, f32[3,2048]{1,0:T(4,128)}, f32[20,2048]{1,0:T(8,128)}) custom-call(s32[1,8,32]{2,1,0:T(8,128)S(1)} %copy-done.4, s32[1,8,32]{2,1,0:T(8,128)S(1)} %copy-done.5, bf16[8,48,128]{2,1,0:T(8,128)(2,1)S(1)} %get-tuple-element.9.flux_ref, bf16[1,8,64,2048]{3,2,1,0:T(8,128)(2,1)S(1)} %copy-done, ...), custom_call_target="tpu_custom_call" | custom-call | tf_op jit(solution)/shard_map/back/pallas_call | solution.py:373
Async XLA Ops:
  0.6 65.7 %copy-start.5 = (s32[1,8,32]{2,1,0:T(8,128)S(1)}, s32[1,8,32]{2,1,0:T(8,128)}, u32[]{:S(2)}) copy-start(s32[1,8,32]{2,1,0:T(8,128)} %dst_hbm.3) | copy-start | bytes 3076
  0.6 65.7 %copy-start.4 = (s32[1,8,32]{2,1,0:T(8,128)S(1)}, s32[1,8,32]{2,1,0:T(8,128)}, u32[]{:S(2)}) copy-start(s32[1,8,32]{2,1,0:T(8,128)} %src_hbm.3) | copy-start | bytes 3076
  0.7 65.7 %copy-start = (bf16[1,8,64,2048]{3,2,1,0:T(8,128)(2,1)S(1)}, bf16[1,8,64,2048]{3,2,1,0:T(8,128)(2,1)}, u32[]{:S(2)}) copy-start(bf16[1,8,64,2048]{3,2,1,0:T(8,128)(2,1)} %w_ref.1) | copy-start | bytes 6291460
  0.7 5.2 %copy-start.1 = (s32[2048,6]{0,1:T(8,128)S(1)}, s32[2048,6]{0,1:T(8,128)}, u32[]{:S(2)}) copy-start(s32[2048,6]{0,1:T(8,128)} %param.21) | copy-start | bytes 147460
  0.7 5.2 %copy-start.8 = (f32[20]{0:T(128)S(1)}, f32[20]{0:T(128)}, u32[]{:S(2)}) copy-start(f32[20]{0:T(128)} %level_weights.1) | copy-start | bytes 244
  0.7 5.2 %copy-start.7 = (f32[2048]{0:T(1024)S(1)}, f32[2048]{0:T(1024)}, u32[]{:S(2)}) copy-start(f32[2048]{0:T(1024)} %param.19) | copy-start | bytes 24580
  0.7 5.2 %copy-start.3 = (bf16[3,2048]{1,0:T(4,128)(2,1)S(1)}, bf16[3,2048]{1,0:T(4,128)(2,1)}, u32[]{:S(2)}) copy-start(bf16[3,2048]{1,0:T(4,128)(2,1)} %ocean_state.1) | copy-start | bytes 36868
  0.7 5.2 %copy-start.2 = (bf16[3,2048]{1,0:T(4,128)(2,1)S(1)}, bf16[3,2048]{1,0:T(4,128)(2,1)}, u32[]{:S(2)}) copy-start(bf16[3,2048]{1,0:T(4,128)(2,1)} %ice_flux.1) | copy-start | bytes 36868
  0.7 5.2 %copy-start.6 = (f32[2048]{0:T(1024)S(1)}, f32[2048]{0:T(1024)}, u32[]{:S(2)}) copy-start(f32[2048]{0:T(1024)} %param.16) | copy-start | bytes 24580

commit v3 on v2

--- a/solution.py
+++ b/solution.py
@@ -75,7 +75,7 @@
     grp_n, dom_n, lev_n,
     agg, ice_cover, ice_flux, ocean_state, drag, level_weights, neighbours,
     surf_out, lev_out, flux_out,
-    sib, comb, recv, own, halo, named, hits, counts, around, ice8, state8, lw_rows, surf8, flat, flux_send, flux_recv, col_send, col_recv,
+    sib, comb, recv, own, halo, tile_of, place_of, counts, around, ice8, state8, lw_rows, flat, flux_send, flux_recv, col_send, col_recv,
     sib_s, sib_r, far_s, far_r, halo_s, halo_r, col_s, col_r, flux_s, flux_r,
 ):
     grp, dom, lev = lax.axis_index("grp"), lax.axis_index("dom"), lax.axis_index("lev")
@@ -101,7 +101,7 @@
 
     barrier = pltpu.get_barrier_semaphore()
     greeted = 0
-    for by in range(1, near + 1):
+    for by in range(1, near):
         for sign in (1, -1):
             pl.semaphore_signal(barrier, inc=1, device_id=part(sign * by), device_id_type=MESH)
             greeted += 1
@@ -111,6 +111,19 @@
     for by in range(1, lev_n):
         pl.semaphore_signal(barrier, inc=1, device_id=column_peer(by), device_id_type=MESH)
         greeted += 1
+    first = levels - 16
+    ice8[...] = jnp.zeros_like(ice8)
+    state8[...] = jnp.zeros_like(state8)
+    ice8[first : first + surf, :] = ice_flux[...].astype(F32)
+    state8[first : first + surf, :] = ocean_state[...].astype(F32)
+    lw_rows[...] = jnp.zeros_like(lw_rows)
+    for k in range(levels):
+        lw_rows[k : k + 1, :] = jnp.full((1, 128), level_weights[k], F32)
+    nb = neighbours.shape[0]
+    place = neighbours[...] - HW
+    place = jnp.where(place < 0, place + cells + 2 * HW, place)
+    tile_of[...] = place >> 7
+    place_of[...] = place & 127
     pl.semaphore_wait(barrier, greeted)
 
     def copy(src, dst, send, got, device):
@@ -138,47 +151,29 @@
     comb[0] = (wide(agg, 2) + wide(sib, core)).astype(BF16)
     far1.start()
 
-    nb = named.shape[0]
-    ext_tiles = counts.shape[0] // 128
-    place = neighbours[...] - HW
-    named[...] = jnp.where(place < 0, place + cells + 2 * HW, place)
-
-    def hit_rows(h, carry):
-        for e in range(nb):
-            hit = jnp.where(jnp.broadcast_to(named[e : e + 1, :] // 128, (16, cells)) == h, 1.0, 0.0)
-            hits[e, pl.ds(pl.multiple_of(h * 16, 16), 16), :] = hit.astype(BF16)
-        return carry
-
     def count_cells(n, carry):
         lanes = pl.ds(pl.multiple_of(n * 128, 128), 128)
-        rows = [jnp.broadcast_to(named[e : e + 1, lanes] % 128, (16, 128)) for e in range(nb)]
-
-        def block(lb, carry):
-            row = lax.broadcasted_iota(jnp.int32, (16, 128), 0) + lb * 16
-            spots = [jnp.where(rows[e] == row, 1.0, 0.0).astype(BF16) for e in range(nb)]
-            for h in range(ext_tiles):
-                total = spots[0] * hits[0, h * 16 : h * 16 + 16, lanes]
-                for e in range(1, nb):
-                    total = total + spots[e] * hits[e, h * 16 : h * 16 + 16, lanes]
-                counts[pl.ds(pl.multiple_of(h * 128 + lb * 16, 16), 16), lanes] = total
-            return carry
-
-        return lax.fori_loop(0, 8, block, carry)
-
-    lax.fori_loop(0, ext_tiles, hit_rows, 0)
+        row = lax.broadcasted_iota(jnp.int32, (128, 128), 0)
+        spots, tile_rows = [], []
+        for e in range(nb):
+            spot = jnp.where(jnp.broadcast_to(place_of[e : e + 1, lanes], (128, 128)) == row, 1.0, 0.0)
+            spots.append(spot.astype(BF16))
+            tile_rows.append(jnp.broadcast_to(tile_of[e : e + 1, lanes], (16, 128)).astype(F32).astype(BF16))
+        for h in range(counts.shape[0] // 128):
+            total = None
+            for e in range(nb):
+                hit = tile_rows[e] == jnp.full((16, 128), h, BF16)
+                term = jnp.where(jnp.concatenate([hit] * 8, axis=0), spots[e], jnp.zeros_like(spots[e]))
+                total = term if total is None else total + term
+            counts[h * 128 : h * 128 + 128, lanes] = total
+        return carry
+
+    early = 3 * tiles // 8
+    lax.fori_loop(0, early, count_cells, 0)
     far3.wait_recv()
     comb[1] = (wide(agg, 4) + wide(sib, 1 + core) + wide(recv, 2)).astype(BF16)
     far2.start()
-    lax.fori_loop(0, tiles, count_cells, 0)
-
-    first = levels - 16
-    ice8[...] = jnp.zeros_like(ice8)
-    state8[...] = jnp.zeros_like(state8)
-    ice8[first : first + surf, :] = ice_flux[...].astype(F32)
-    state8[first : first + surf, :] = ocean_state[...].astype(F32)
-    lw_rows[...] = jnp.zeros_like(lw_rows)
-    for k in range(levels):
-        lw_rows[k : k + 1, :] = jnp.full((1, 128), level_weights[k], F32)
+    lax.fori_loop(early, tiles, count_cells, 0)
 
     far1.wait_recv()
     far2.wait_recv()
@@ -204,26 +199,25 @@
         around[:, lanes] = dot(own[...], counts[0:cells, lanes])
     to_prev.wait_recv()
     to_next.wait_recv()
+    weight = jnp.concatenate([lw_rows[...], lw_rows[...]], axis=1)
     for c in range(cells // 256):
         lanes = slice(c * 256, c * 256 + 256)
         total = around[:, lanes] + dot(halo[...], counts[cells : cells + 2 * HW, lanes])
-        forcing = (1.0 - KAPPA) * own[:, lanes].astype(F32) + (KAPPA / named.shape[0]) * total
-        forcing = forcing[:ROWS]
-        lev_out[:, lanes] = forcing[:levels]
-        surf_out[:, lanes] = forcing[levels : levels + surf]
-        surf8[:, lanes] = forcing[16:]
-        weight = jnp.concatenate([lw_rows[...], lw_rows[...]], axis=1)
-        col_send[:, lanes] = jnp.sum(weight * forcing, axis=0, keepdims=True)
+        forcing = (1.0 - KAPPA) * own[:, lanes].astype(F32) + (KAPPA / nb) * total
+        around[:, lanes] = forcing
+        col_send[:, lanes] = jnp.sum(weight * forcing[:ROWS], axis=0, keepdims=True)
 
     col_copies = [copy(col_send, col_recv.at[by - 1], col_s.at[by - 1], col_r.at[by - 1], column_peer(by)) for by in range(1, lev_n)]
     for one in col_copies:
         one.start()
+    lev_out[...] = around[:levels, :]
+    surf_out[...] = around[levels : levels + surf, :]
     for one in col_copies:
         one.wait_recv()
     column = col_send[...]
     for by in range(1, lev_n):
         column = column + col_recv[by - 1]
-    flux = drag[...] * (state8[...] - surf8[...] + column)
+    flux = drag[...] * (state8[...] - around[16:ROWS, :] + column)
     for t in range(tiles):
         flat[t * surf : (t + 1) * surf, :] = flux[first : first + surf, t * 128 : t * 128 + 128]
     flux_send[...] = flat[...].astype(BF16)
@@ -348,13 +342,12 @@
             pltpu.VMEM((32, cells), BF16),
             pltpu.VMEM((32, 2 * HW), BF16),
             pltpu.VMEM((neighbours.shape[1], cells), jnp.int32),
-            pltpu.VMEM((neighbours.shape[1], (cells + 2 * HW) // 8, cells), BF16),
+            pltpu.VMEM((neighbours.shape[1], cells), jnp.int32),
             pltpu.VMEM((cells + 2 * HW, cells), BF16),
             pltpu.VMEM((32, cells), F32),
             pltpu.VMEM((8, cells), F32),
             pltpu.VMEM((8, cells), F32),
             pltpu.VMEM((ROWS, 128), F32),
-            pltpu.VMEM((8, cells), F32),
             pltpu.VMEM((tiles * surf, 128), F32),
             pltpu.VMEM((tiles * surf, 128), BF16),
             pltpu.VMEM((near - 1, tiles * surf, 128), BF16),

time: 70.3 us -> 57.7 us (0.82)
  Pallas kernels: 69.3 us -> 56.8 us
    pallas_call x1, Pallas kernels: 60.4 us -> 47.9 us  [shards(): pl.pallas_call(functools.partial(middle_kernel, grp_n, dom_n, lev_n), out...]
where the time goes in v3:
time: 57.7 us; the launch traced here: 57.6 us
  Pallas kernels  56.8 us (98%)
  between operations  0.79 us (1%)
    pallas_call x1, Pallas kernels, shards(): pl.pallas_call(functools.partial(middle_kernel, grp_n, dom_n, lev_n), out...  47.9 us
    pallas_call x1, Pallas kernels, shards(): pl.pallas_call(forward_kernel, out_shape=jax.ShapeDtypeStruct((near, flat...  5.07 us
    pallas_call x1, Pallas kernels, shards(): pl.pallas_call(back_kernel, out_shape=[jax.ShapeDtypeStruct((surf, column...  3.82 us

profile of v3, /device:TPU:1, one launch (start us, length us, event | category | flops | bytes accessed | tf_op | source)
XLA Modules:
  0.0 57.6 jit_solution(16140694605624204449)
XLA Ops:
  0.6 0.0 copy-start.5
  0.6 0.0 copy-start.4
  0.7 0.0 copy-start
  0.7 0.0 copy-start.1
  0.7 0.0 copy-start.8
  0.7 0.0 copy-start.7
  0.7 0.0 copy-start.3
  0.7 0.0 copy-start.2
  0.7 0.0 copy-start.6
  0.7 5.1 %pieces.1.agg = bf16[8,384,128]{2,1,0:T(8,128)(2,1)S(1)} custom-call(s32[1,8,32]{2,1,0:T(8,128)} %src_hbm.3, s32[1,8,32]{2,1,0:T(8,128)} %dst_hbm.3, bf16[3,4096]{1,0:T(4,128)(2,1)} %surf_hbm.1, bf16[20,4096]{1,0:T(8,128)(2,1)} %lev_hbm.1, bf16[1,8,64,2048]{3,2,1,0:T(8,128)(2,1)} %w_ref.1), custom_call_target="tpu_custom_call" | custom-call | tf_op jit(solution)/shard_map/pieces/pallas_call | solution.py:306
  5.8 0.0 copy-done.1
  5.8 0.0 copy-done.8
  5.8 0.0 copy-done.7
  5.8 0.0 copy-done.3
  5.8 0.0 copy-done.2
  5.9 0.0 copy-done.6
  5.9 47.9 %middle.1 = (f32[3,2048]{1,0:T(4,128)S(1)}, f32[20,2048]{1,0:T(8,128)S(1)}, bf16[8,48,128]{2,1,0:T(8,128)(2,1)S(1)}) custom-call(bf16[8,384,128]{2,1,0:T(8,128)(2,1)S(1)} %pieces.1.agg, f32[1,2048]{1,0:T(1,128)S(1)} %bitcast.4, bf16[3,2048]{1,0:T(4,128)(2,1)S(1)} %copy-done.2, bf16[3,2048]{1,0:T(4,128)(2,1)S(1)} %copy-done.3, f32[1,2048]{1,0:T(1,128)S(1)} %bitcast.5, ...), custom_call_target="tpu_custom_call" | custom-call | tf_op jit(solution)/shard_map/middle/pallas_call | solution.py:329
  53.8 0.0 copy-done.5
  53.8 0.0 copy-done.4
  53.8 0.0 copy-done
  53.8 3.8 %back.1 = (f32[3,4096]{1,0:T(4,128)}, f32[3,2048]{1,0:T(4,128)}, f32[20,2048]{1,0:T(8,128)}) custom-call(s32[1,8,32]{2,1,0:T(8,128)S(1)} %copy-done.4, s32[1,8,32]{2,1,0:T(8,128)S(1)} %copy-done.5, bf16[8,48,128]{2,1,0:T(8,128)(2,1)S(1)} %get-tuple-element.9.flux_ref, bf16[1,8,64,2048]{3,2,1,0:T(8,128)(2,1)S(1)} %copy-done, ...), custom_call_target="tpu_custom_call" | custom-call | tf_op jit(solution)/shard_map/back/pallas_call | solution.py:366
Async XLA Ops:
  0.6 53.1 %copy-start.5 = (s32[1,8,32]{2,1,0:T(8,128)S(1)}, s32[1,8,32]{2,1,0:T(8,128)}, u32[]{:S(2)}) copy-start(s32[1,8,32]{2,1,0:T(8,128)} %dst_hbm.3) | copy-start | bytes 3076
  0.6 53.1 %copy-start.4 = (s32[1,8,32]{2,1,0:T(8,128)S(1)}, s32[1,8,32]{2,1,0:T(8,128)}, u32[]{:S(2)}) copy-start(s32[1,8,32]{2,1,0:T(8,128)} %src_hbm.3) | copy-start | bytes 3076
  0.7 53.1 %copy-start = (bf16[1,8,64,2048]{3,2,1,0:T(8,128)(2,1)S(1)}, bf16[1,8,64,2048]{3,2,1,0:T(8,128)(2,1)}, u32[]{:S(2)}) copy-start(bf16[1,8,64,2048]{3,2,1,0:T(8,128)(2,1)} %w_ref.1) | copy-start | bytes 6291460
  0.7 5.1 %copy-start.1 = (s32[2048,6]{0,1:T(8,128)S(1)}, s32[2048,6]{0,1:T(8,128)}, u32[]{:S(2)}) copy-start(s32[2048,6]{0,1:T(8,128)} %param.21) | copy-start | bytes 147460
  0.7 5.1 %copy-start.8 = (f32[20]{0:T(128)S(1)}, f32[20]{0:T(128)}, u32[]{:S(2)}) copy-start(f32[20]{0:T(128)} %level_weights.1) | copy-start | bytes 244
  0.7 5.1 %copy-start.7 = (f32[2048]{0:T(1024)S(1)}, f32[2048]{0:T(1024)}, u32[]{:S(2)}) copy-start(f32[2048]{0:T(1024)} %param.19) | copy-start | bytes 24580
  0.7 5.1 %copy-start.3 = (bf16[3,2048]{1,0:T(4,128)(2,1)S(1)}, bf16[3,2048]{1,0:T(4,128)(2,1)}, u32[]{:S(2)}) copy-start(bf16[3,2048]{1,0:T(4,128)(2,1)} %ocean_state.1) | copy-start | bytes 36868
  0.7 5.1 %copy-start.2 = (bf16[3,2048]{1,0:T(4,128)(2,1)S(1)}, bf16[3,2048]{1,0:T(4,128)(2,1)}, u32[]{:S(2)}) copy-start(bf16[3,2048]{1,0:T(4,128)(2,1)} %ice_flux.1) | copy-start | bytes 36868
  0.7 5.1 %copy-start.6 = (f32[2048]{0:T(1024)S(1)}, f32[2048]{0:T(1024)}, u32[]{:S(2)}) copy-start(f32[2048]{0:T(1024)} %param.16) | copy-start | bytes 24580

commit v4 on v3

--- a/solution.py
+++ b/solution.py
@@ -75,8 +75,8 @@
     grp_n, dom_n, lev_n,
     agg, ice_cover, ice_flux, ocean_state, drag, level_weights, neighbours,
     surf_out, lev_out, flux_out,
-    sib, comb, recv, own, halo, tile_of, place_of, counts, around, ice8, state8, lw_rows, flat, flux_send, flux_recv, col_send, col_recv,
-    sib_s, sib_r, far_s, far_r, halo_s, halo_r, col_s, col_r, flux_s, flux_r,
+    sib, comb, recv, own, parts_of, tile_of, place_of, counts, around, ice8, state8, lw_rows, flat, flux_send, flux_recv, col_send, col_recv, edge_recv,
+    sib_s, sib_r, far_s, far_r, halo_s, halo_r, col_s, col_r, edge_s, edge_r, flux_s, flux_r,
 ):
     grp, dom, lev = lax.axis_index("grp"), lax.axis_index("dom"), lax.axis_index("lev")
     parts = grp_n * dom_n
@@ -91,11 +91,8 @@
         q = lax.rem(p + by + parts, parts)
         return (q // dom_n, lax.rem(q, dom_n), lev)
 
-    def ring(by):
-        return (grp, lax.rem(dom + by + dom_n, dom_n), lev)
-
-    def column_peer(by):
-        return (grp, dom, lax.rem(lev + by, lev_n))
+    def ring(by, over=0):
+        return (grp, lax.rem(dom + by + dom_n, dom_n), lax.rem(lev + over, lev_n))
 
     sibling = (grp, dom + 1 - 2 * core, lev)
 
@@ -108,9 +105,10 @@
     for by in (1, -1):
         pl.semaphore_signal(barrier, inc=1, device_id=ring(by), device_id_type=MESH)
         greeted += 1
-    for by in range(1, lev_n):
-        pl.semaphore_signal(barrier, inc=1, device_id=column_peer(by), device_id_type=MESH)
-        greeted += 1
+    for over in range(1, lev_n):
+        for by in (0, 1, -1):
+            pl.semaphore_signal(barrier, inc=1, device_id=ring(by, over), device_id_type=MESH)
+            greeted += 1
     first = levels - 16
     ice8[...] = jnp.zeros_like(ice8)
     state8[...] = jnp.zeros_like(state8)
@@ -188,48 +186,58 @@
             one = total[u * ROWS : (u + 1) * ROWS]
             share = ice_cover[:, lanes]
             tail = jnp.where(is_surf, (1.0 - share) * one[16:] + share * ice8[:, lanes], one[16:])
-            own[:, lanes] = jnp.concatenate([one[:16], tail, jnp.zeros((8, 128), F32)], axis=0).astype(BF16)
-
-    to_prev = copy(own.at[:, 0:HW], halo.at[:, 0:HW], halo_s.at[0], halo_r.at[0], ring(-1))
-    to_next = copy(own.at[:, cells - HW : cells], halo.at[:, HW : 2 * HW], halo_s.at[1], halo_r.at[1], ring(1))
-    to_prev.start()
-    to_next.start()
+            merged = jnp.concatenate([one[:16], tail, jnp.zeros((8, 128), F32)], axis=0).astype(BF16)
+            own[:, lanes] = merged
+            col_send[:, lanes] = jnp.sum(lw_rows[...] * merged.astype(F32)[:ROWS], axis=0, keepdims=True)
+
+    first_cells, last_cells = slice(0, HW), slice(cells - HW, cells)
+    border = [
+        copy(own.at[:, first_cells], own.at[:, cells : cells + HW], halo_s.at[0], halo_r.at[0], ring(-1)),
+        copy(own.at[:, last_cells], own.at[:, cells + HW : cells + 2 * HW], halo_s.at[1], halo_r.at[1], ring(1)),
+    ]
+    for over in range(1, lev_n):
+        border.append(copy(col_send, col_recv.at[over - 1], col_s.at[over - 1], col_r.at[over - 1], ring(0, over)))
+    for over in range(lev_n):
+        to, up = over, lev_n + over
+        border.append(copy(col_send.at[:, first_cells], edge_recv.at[to], edge_s.at[to], edge_r.at[to], ring(-1, over)))
+        border.append(copy(col_send.at[:, last_cells], edge_recv.at[up], edge_s.at[up], edge_r.at[up], ring(1, over)))
+    for one in border:
+        one.start()
+    for one in border:
+        one.wait_recv()
+    inner, after, before = col_send[...], edge_recv[0], edge_recv[lev_n]
+    for over in range(1, lev_n):
+        inner = inner + col_recv[over - 1]
+        after = after + edge_recv[over]
+        before = before + edge_recv[lev_n + over]
+    inner = jnp.concatenate([inner, after, before], axis=1)
+    high = inner.astype(BF16).astype(F32)
+    middle = (inner - high).astype(BF16).astype(F32)
+    row = lax.broadcasted_iota(jnp.int32, (16, cells + 2 * HW), 0)
+    split = jnp.where(row == 0, high, jnp.where(row == 1, middle, jnp.where(row == 2, inner - high - middle, 0.0)))
+    parts_of[...] = split.astype(BF16)
     for c in range(cells // 256):
         lanes = slice(c * 256, c * 256 + 256)
-        around[:, lanes] = dot(own[...], counts[0:cells, lanes])
-    to_prev.wait_recv()
-    to_next.wait_recv()
-    weight = jnp.concatenate([lw_rows[...], lw_rows[...]], axis=1)
-    for c in range(cells // 256):
-        lanes = slice(c * 256, c * 256 + 256)
-        total = around[:, lanes] + dot(halo[...], counts[cells : cells + 2 * HW, lanes])
-        forcing = (1.0 - KAPPA) * own[:, lanes].astype(F32) + (KAPPA / nb) * total
+        total = dot(jnp.concatenate([own[...], parts_of[...]], axis=0), counts[:, lanes])
+        forcing = (1.0 - KAPPA) * own[:, lanes].astype(F32) + (KAPPA / nb) * total[:32]
         around[:, lanes] = forcing
-        col_send[:, lanes] = jnp.sum(weight * forcing[:ROWS], axis=0, keepdims=True)
-
-    col_copies = [copy(col_send, col_recv.at[by - 1], col_s.at[by - 1], col_r.at[by - 1], column_peer(by)) for by in range(1, lev_n)]
-    for one in col_copies:
-        one.start()
-    lev_out[...] = around[:levels, :]
-    surf_out[...] = around[levels : levels + surf, :]
-    for one in col_copies:
-        one.wait_recv()
-    column = col_send[...]
-    for by in range(1, lev_n):
-        column = column + col_recv[by - 1]
-    flux = drag[...] * (state8[...] - around[16:ROWS, :] + column)
-    for t in range(tiles):
-        flat[t * surf : (t + 1) * surf, :] = flux[first : first + surf, t * 128 : t * 128 + 128]
+        column = (1.0 - KAPPA) * inner[:, lanes] + (KAPPA / nb) * (total[32:33] + total[33:34] + total[34:35])
+        flux = drag[:, lanes] * (state8[:, lanes] - forcing[16:ROWS] + column)
+        for u in range(2):
+            t = 2 * c + u
+            flat[t * surf : (t + 1) * surf, :] = flux[first : first + surf, u * 128 : u * 128 + 128]
     flux_send[...] = flat[...].astype(BF16)
     flux_copies = [copy(flux_send, flux_recv.at[o - 1], flux_s.at[o - 1], flux_r.at[o - 1], part(-o)) for o in range(1, near)]
     for one in reversed(flux_copies):
         one.start()
+    lev_out[...] = around[:levels, :]
+    surf_out[...] = around[levels : levels + surf, :]
     flux_out[0] = flux_send[...]
     for o in range(1, near):
         flux_copies[o - 1].wait_recv()
         flux_out[o] = flux_recv[o - 1]
 
-    for one in sib_copies + [far1, far2, far3, to_prev, to_next] + col_copies + flux_copies:
+    for one in sib_copies + [far1, far2, far3] + border + flux_copies:
         one.wait_send()
 
 
@@ -339,8 +347,8 @@
             pltpu.VMEM((4, flat_rows, 128), BF16),
             pltpu.VMEM((3, flat_rows, 128), BF16),
             pltpu.VMEM((3, flat_rows, 128), BF16),
-            pltpu.VMEM((32, cells), BF16),
-            pltpu.VMEM((32, 2 * HW), BF16),
+            pltpu.VMEM((32, cells + 2 * HW), BF16),
+            pltpu.VMEM((16, cells + 2 * HW), BF16),
             pltpu.VMEM((neighbours.shape[1], cells), jnp.int32),
             pltpu.VMEM((neighbours.shape[1], cells), jnp.int32),
             pltpu.VMEM((cells + 2 * HW, cells), BF16),
@@ -353,10 +361,12 @@
             pltpu.VMEM((near - 1, tiles * surf, 128), BF16),
             pltpu.VMEM((1, cells), F32),
             pltpu.VMEM((max(lev_n - 1, 1), 1, cells), F32),
+            pltpu.VMEM((2 * lev_n, 1, HW), F32),
             dma((4,)), dma((4,)),
             dma((3,)), dma((3,)),
             dma((2,)), dma((2,)),
-            dma((3,)), dma((3,)),
+            dma((max(lev_n - 1, 1),)), dma((max(lev_n - 1, 1),)),
+            dma((2 * lev_n,)), dma((2 * lev_n,)),
             dma((near - 1,)), dma((near - 1,)),
         ],
         compiler_params=pltpu.CompilerParams(collective_id=0, has_side_effects=True, vmem_limit_bytes=48 * 2**20),

time: 57.7 us -> 58.7 us (1.017)
  Pallas kernels: 56.8 us -> 57.7 us
    pallas_call x1, Pallas kernels: 47.9 us -> 48.8 us  [shards(): pl.pallas_call(functools.partial(middle_kernel, grp_n, dom_n, lev_n), out...]
where the time goes in v4:
time: 58.7 us; the launch traced here: 58.5 us
  Pallas kernels  57.7 us (98%)
  between operations  0.79 us (1%)
    pallas_call x1, Pallas kernels, shards(): pl.pallas_call(functools.partial(middle_kernel, grp_n, dom_n, lev_n), out...  48.8 us
    pallas_call x1, Pallas kernels, shards(): pl.pallas_call(forward_kernel, out_shape=jax.ShapeDtypeStruct((near, flat...  5.09 us
    pallas_call x1, Pallas kernels, shards(): pl.pallas_call(back_kernel, out_shape=[jax.ShapeDtypeStruct((surf, column...  3.84 us

profile of v4, /device:TPU:1, one launch (start us, length us, event | category | flops | bytes accessed | tf_op | source)
XLA Modules:
  0.0 58.5 jit_solution(16232389020804028094)
XLA Ops:
  0.6 0.0 copy-start.5
  0.6 0.0 copy-start.4
  0.7 0.0 copy-start
  0.7 0.0 copy-start.1
  0.7 0.0 copy-start.8
  0.7 0.0 copy-start.7
  0.7 0.0 copy-start.3
  0.7 0.0 copy-start.2
  0.7 0.0 copy-start.6
  0.7 5.1 %pieces.1.agg = bf16[8,384,128]{2,1,0:T(8,128)(2,1)S(1)} custom-call(s32[1,8,32]{2,1,0:T(8,128)} %src_hbm.3, s32[1,8,32]{2,1,0:T(8,128)} %dst_hbm.3, bf16[3,4096]{1,0:T(4,128)(2,1)} %surf_hbm.1, bf16[20,4096]{1,0:T(8,128)(2,1)} %lev_hbm.1, bf16[1,8,64,2048]{3,2,1,0:T(8,128)(2,1)} %w_ref.1), custom_call_target="tpu_custom_call" | custom-call | tf_op jit(solution)/shard_map/pieces/pallas_call | solution.py:314
  5.8 0.0 copy-done.1
  5.8 0.0 copy-done.8
  5.8 0.0 copy-done.7
  5.8 0.0 copy-done.3
  5.9 0.0 copy-done.2
  5.9 0.0 copy-done.6
  5.9 48.8 %middle.1 = (f32[3,2048]{1,0:T(4,128)S(1)}, f32[20,2048]{1,0:T(8,128)S(1)}, bf16[8,48,128]{2,1,0:T(8,128)(2,1)S(1)}) custom-call(bf16[8,384,128]{2,1,0:T(8,128)(2,1)S(1)} %pieces.1.agg, f32[1,2048]{1,0:T(1,128)S(1)} %bitcast.4, bf16[3,2048]{1,0:T(4,128)(2,1)S(1)} %copy-done.2, bf16[3,2048]{1,0:T(4,128)(2,1)S(1)} %copy-done.3, f32[1,2048]{1,0:T(1,128)S(1)} %bitcast.5, ...), custom_call_target="tpu_custom_call" | custom-call | tf_op jit(solution)/shard_map/middle/pallas_call | solution.py:337
  54.7 0.0 copy-done.5
  54.7 0.0 copy-done.4
  54.7 0.0 copy-done
  54.7 3.8 %back.1 = (f32[3,4096]{1,0:T(4,128)}, f32[3,2048]{1,0:T(4,128)}, f32[20,2048]{1,0:T(8,128)}) custom-call(s32[1,8,32]{2,1,0:T(8,128)S(1)} %copy-done.4, s32[1,8,32]{2,1,0:T(8,128)S(1)} %copy-done.5, bf16[8,48,128]{2,1,0:T(8,128)(2,1)S(1)} %get-tuple-element.9.flux_ref, bf16[1,8,64,2048]{3,2,1,0:T(8,128)(2,1)S(1)} %copy-done, ...), custom_call_target="tpu_custom_call" | custom-call | tf_op jit(solution)/shard_map/back/pallas_call | solution.py:376
Async XLA Ops:
  0.6 54.0 %copy-start.5 = (s32[1,8,32]{2,1,0:T(8,128)S(1)}, s32[1,8,32]{2,1,0:T(8,128)}, u32[]{:S(2)}) copy-start(s32[1,8,32]{2,1,0:T(8,128)} %dst_hbm.3) | copy-start | bytes 3076
  0.6 54.0 %copy-start.4 = (s32[1,8,32]{2,1,0:T(8,128)S(1)}, s32[1,8,32]{2,1,0:T(8,128)}, u32[]{:S(2)}) copy-start(s32[1,8,32]{2,1,0:T(8,128)} %src_hbm.3) | copy-start | bytes 3076
  0.7 54.0 %copy-start = (bf16[1,8,64,2048]{3,2,1,0:T(8,128)(2,1)S(1)}, bf16[1,8,64,2048]{3,2,1,0:T(8,128)(2,1)}, u32[]{:S(2)}) copy-start(bf16[1,8,64,2048]{3,2,1,0:T(8,128)(2,1)} %w_ref.1) | copy-start | bytes 6291460
  0.7 5.2 %copy-start.1 = (s32[2048,6]{0,1:T(8,128)S(1)}, s32[2048,6]{0,1:T(8,128)}, u32[]{:S(2)}) copy-start(s32[2048,6]{0,1:T(8,128)} %param.21) | copy-start | bytes 147460
  0.7 5.2 %copy-start.8 = (f32[20]{0:T(128)S(1)}, f32[20]{0:T(128)}, u32[]{:S(2)}) copy-start(f32[20]{0:T(128)} %level_weights.1) | copy-start | bytes 244
  0.7 5.2 %copy-start.7 = (f32[2048]{0:T(1024)S(1)}, f32[2048]{0:T(1024)}, u32[]{:S(2)}) copy-start(f32[2048]{0:T(1024)} %param.19) | copy-start | bytes 24580
  0.7 5.2 %copy-start.3 = (bf16[3,2048]{1,0:T(4,128)(2,1)S(1)}, bf16[3,2048]{1,0:T(4,128)(2,1)}, u32[]{:S(2)}) copy-start(bf16[3,2048]{1,0:T(4,128)(2,1)} %ocean_state.1) | copy-start | bytes 36868
  0.7 5.2 %copy-start.2 = (bf16[3,2048]{1,0:T(4,128)(2,1)S(1)}, bf16[3,2048]{1,0:T(4,128)(2,1)}, u32[]{:S(2)}) copy-start(bf16[3,2048]{1,0:T(4,128)(2,1)} %ice_flux.1) | copy-start | bytes 36868
  0.7 5.2 %copy-start.6 = (f32[2048]{0:T(1024)S(1)}, f32[2048]{0:T(1024)}, u32[]{:S(2)}) copy-start(f32[2048]{0:T(1024)} %param.16) | copy-start | bytes 24580

commit v5 on v3

--- a/solution.py
+++ b/solution.py
@@ -111,6 +111,24 @@
     for by in range(1, lev_n):
         pl.semaphore_signal(barrier, inc=1, device_id=column_peer(by), device_id_type=MESH)
         greeted += 1
+    pl.semaphore_wait(barrier, greeted)
+
+    def copy(src, dst, send, got, device):
+        return pltpu.make_async_remote_copy(
+            src_ref=src, dst_ref=dst, send_sem=send, recv_sem=got, device_id=device, device_id_type=MESH
+        )
+
+    sib_copies = [copy(agg.at[2 * m + 1], sib.at[m], sib_s.at[m], sib_r.at[m], sibling) for m in range(3)]
+    sib_copies.append(copy(agg.at[7], sib.at[3], sib_s.at[3], sib_r.at[3], part(1)))
+    far1 = copy(comb.at[0], recv.at[0], far_s.at[0], far_r.at[0], part(2))
+    far2 = copy(comb.at[1], recv.at[1], far_s.at[1], far_r.at[1], part(4))
+    far3 = copy(comb.at[2], recv.at[2], far_s.at[2], far_r.at[2], part(2))
+    for m in reversed(range(4)):
+        sib_copies[m].start()
+
+    def wide(ref, n):
+        return ref[n].astype(F32)
+
     first = levels - 16
     ice8[...] = jnp.zeros_like(ice8)
     state8[...] = jnp.zeros_like(state8)
@@ -124,33 +142,6 @@
     place = jnp.where(place < 0, place + cells + 2 * HW, place)
     tile_of[...] = place >> 7
     place_of[...] = place & 127
-    pl.semaphore_wait(barrier, greeted)
-
-    def copy(src, dst, send, got, device):
-        return pltpu.make_async_remote_copy(
-            src_ref=src, dst_ref=dst, send_sem=send, recv_sem=got, device_id=device, device_id_type=MESH
-        )
-
-    sib_copies = [copy(agg.at[2 * m + 1], sib.at[m], sib_s.at[m], sib_r.at[m], sibling) for m in range(3)]
-    sib_copies.append(copy(agg.at[7], sib.at[3], sib_s.at[3], sib_r.at[3], part(1)))
-    far1 = copy(comb.at[0], recv.at[0], far_s.at[0], far_r.at[0], part(2))
-    far2 = copy(comb.at[1], recv.at[1], far_s.at[1], far_r.at[1], part(4))
-    far3 = copy(comb.at[2], recv.at[2], far_s.at[2], far_r.at[2], part(2))
-    for m in reversed(range(4)):
-        sib_copies[m].start()
-
-    def wide(ref, n):
-        return ref[n].astype(F32)
-
-    sib_copies[3].wait_recv()
-    sib_copies[2].wait_recv()
-    comb[2] = (wide(agg, 6) + wide(sib, 3) + jnp.where(core == 0, wide(sib, 2), 0.0)).astype(BF16)
-    far3.start()
-    sib_copies[1].wait_recv()
-    sib_copies[0].wait_recv()
-    comb[0] = (wide(agg, 2) + wide(sib, core)).astype(BF16)
-    far1.start()
-
     def count_cells(n, carry):
         lanes = pl.ds(pl.multiple_of(n * 128, 128), 128)
         row = lax.broadcasted_iota(jnp.int32, (128, 128), 0)
@@ -168,18 +159,27 @@
             counts[h * 128 : h * 128 + 128, lanes] = total
         return carry
 
-    early = 3 * tiles // 8
-    lax.fori_loop(0, early, count_cells, 0)
+    lax.fori_loop(0, 5 * tiles // 16, count_cells, 0)
+    sib_copies[3].wait_recv()
+    sib_copies[2].wait_recv()
+    comb[2] = (wide(agg, 6) + wide(sib, 3) + jnp.where(core == 0, wide(sib, 2), 0.0)).astype(BF16)
+    far3.start()
+    sib_copies[1].wait_recv()
+    sib_copies[0].wait_recv()
+    comb[0] = (wide(agg, 2) + wide(sib, core)).astype(BF16)
+    far1.start()
+
+    lax.fori_loop(5 * tiles // 16, 5 * tiles // 8, count_cells, 0)
     far3.wait_recv()
     comb[1] = (wide(agg, 4) + wide(sib, 1 + core) + wide(recv, 2)).astype(BF16)
     far2.start()
-    lax.fori_loop(early, tiles, count_cells, 0)
+    lax.fori_loop(5 * tiles // 8, tiles, count_cells, 0)
 
     far1.wait_recv()
     far2.wait_recv()
 
     is_surf = lax.broadcasted_iota(jnp.int32, (8, 128), 0) >= first
-    for t in range(0, tiles, 2):
+    def merge(t):
         rows = slice(t * ROWS, (t + 2) * ROWS)
         total = agg[0, rows, :].astype(F32) + recv[0, rows, :].astype(F32) + recv[1, rows, :].astype(F32)
         total = total + jnp.where(core == 1, sib[0, rows, :].astype(F32), 0.0)
@@ -190,10 +190,14 @@
             tail = jnp.where(is_surf, (1.0 - share) * one[16:] + share * ice8[:, lanes], one[16:])
             own[:, lanes] = jnp.concatenate([one[:16], tail, jnp.zeros((8, 128), F32)], axis=0).astype(BF16)
 
+    merge(0)
+    merge(tiles - 2)
     to_prev = copy(own.at[:, 0:HW], halo.at[:, 0:HW], halo_s.at[0], halo_r.at[0], ring(-1))
     to_next = copy(own.at[:, cells - HW : cells], halo.at[:, HW : 2 * HW], halo_s.at[1], halo_r.at[1], ring(1))
     to_prev.start()
     to_next.start()
+    for t in range(2, tiles - 2, 2):
+        merge(t)
     for c in range(cells // 256):
         lanes = slice(c * 256, c * 256 + 256)
         around[:, lanes] = dot(own[...], counts[0:cells, lanes])
@@ -245,14 +249,14 @@
     for one in copies:
         one.start()
     total[...] = jnp.zeros_like(total)
-    even[...] = jnp.zeros_like(even)
-    odd[...] = jnp.zeros_like(odd)
     low = lax.broadcasted_iota(jnp.int32, (surf, 128), 1) < 64
     zero = jnp.zeros((surf, 128), F32)
     flat[...] = flux_ref[...].astype(F32)
 
     def spread(o, carry):
         base = o * (count + 1)
+        even[base + count] = jnp.zeros((8, 128), F32)
+        odd[base + count] = jnp.zeros((8, 128), F32)
         for t in range(count // 2):
             here = flat[o, t * surf : (t + 1) * surf, :]
             there = pltpu.roll(here, 64, 1)
@@ -268,23 +272,31 @@
 
     def offset(o, carry):
         base = o * (count + 1)
-        for pair in range(slots // 2):
-            a, b = 2 * pair, 2 * pair + 1
-            to_a, to_b = dst[o, a], dst[o, b]
-            to_a = jnp.where(to_a < 0, count, to_a)
-            to_b = jnp.where(to_b < 0, count, to_b)
-            lhs = jnp.concatenate([even[base + to_a], odd[base + to_b]], axis=0).astype(BF16)
+        zero = jnp.zeros((16, 128), BF16)
+        for quad in range(slots // 4):
+            rows = []
+            for half in range(2):
+                to_a, to_b = dst[o, 4 * quad + 2 * half], dst[o, 4 * quad + 2 * half + 1]
+                to_a = jnp.where(to_a < 0, count, to_a)
+                to_b = jnp.where(to_b < 0, count, to_b)
+                rows.append(jnp.concatenate([even[base + to_a], odd[base + to_b]], axis=0).astype(BF16))
+            lhs = jnp.concatenate(
+                [jnp.concatenate([rows[0], zero], axis=1), jnp.concatenate([zero, rows[1]], axis=1)], axis=0
+            )
             got = lax.dot_general(
-                lhs, w_ref[0, o, :, pair * 128 : pair * 128 + 128], (((1,), (1,)), ((), ())), preferred_element_type=F32
+                lhs, w_ref[0, o, :, quad * 256 : quad * 256 + 256], (((1,), (1,)), ((), ())), preferred_element_type=F32
             )
-            from_a, from_b = src[o, a], src[o, b]
-            total[from_a] = total[from_a] + got[:8]
-            total[from_b] = total[from_b] + got[8:]
+            for u in range(4):
+                to = src[o, 4 * quad + u]
+                total[u, to] = total[u, to] + got[8 * u : 8 * u + 8]
         return carry
 
     lax.fori_loop(0, near, offset, 0)
-    for pair in range(total.shape[0] // 2):
-        both = jnp.concatenate([total[2 * pair], total[2 * pair + 1]], axis=1)
+    def summed(b):
+        return (total[0, b] + total[1, b]) + (total[2, b] + total[3, b])
+
+    for pair in range(total.shape[1] // 2):
+        both = jnp.concatenate([summed(2 * pair), summed(2 * pair + 1)], axis=1)
         out_ref[:, pair * 128 : pair * 128 + 128] = both[:surf]
     copies[2].wait()
     copies[3].wait()
@@ -378,7 +390,7 @@
             pltpu.VMEM((near, tiles * surf, 128), F32),
             pltpu.VMEM((near * (cells // width + 1), 8, 128), F32),
             pltpu.VMEM((near * (cells // width + 1), 8, 128), F32),
-            pltpu.VMEM((columns // width, 8, width), F32),
+            pltpu.VMEM((4, columns // width, 8, width), F32),
             dma((4,)),
         ],
         compiler_params=pltpu.CompilerParams(vmem_limit_bytes=32 * 2**20),

time: 57.7 us -> 57.3 us (level)
  no operation moved by 1% of the time
where the time goes in v5:
time: 57.3 us; the launch traced here: 57.2 us
  Pallas kernels  56.3 us (98%)
  between operations  0.79 us (1%)
    pallas_call x1, Pallas kernels, shards(): pl.pallas_call(functools.partial(middle_kernel, grp_n, dom_n, lev_n), out...  47.7 us
    pallas_call x1, Pallas kernels, shards(): pl.pallas_call(forward_kernel, out_shape=jax.ShapeDtypeStruct((near, flat...  5.1 us
    pallas_call x1, Pallas kernels, shards(): pl.pallas_call(back_kernel, out_shape=[jax.ShapeDtypeStruct((surf, column...  3.58 us

profile of v5, /device:TPU:1, one launch (start us, length us, event | category | flops | bytes accessed | tf_op | source)
XLA Modules:
  0.0 57.2 jit_solution(8245192885956614634)
XLA Ops:
  0.6 0.0 copy-start.5
  0.6 0.0 copy-start.4
  0.7 0.0 copy-start
  0.7 0.0 copy-start.1
  0.7 0.0 copy-start.8
  0.7 0.0 copy-start.7
  0.7 0.0 copy-start.3
  0.7 0.0 copy-start.2
  0.7 0.0 copy-start.6
  0.7 5.1 %pieces.1.agg = bf16[8,384,128]{2,1,0:T(8,128)(2,1)S(1)} custom-call(s32[1,8,32]{2,1,0:T(8,128)} %src_hbm.3, s32[1,8,32]{2,1,0:T(8,128)} %dst_hbm.3, bf16[3,4096]{1,0:T(4,128)(2,1)} %surf_hbm.1, bf16[20,4096]{1,0:T(8,128)(2,1)} %lev_hbm.1, bf16[1,8,64,2048]{3,2,1,0:T(8,128)(2,1)} %w_ref.1), custom_call_target="tpu_custom_call" | custom-call | tf_op jit(solution)/shard_map/pieces/pallas_call | solution.py:318
  5.8 0.0 copy-done.1
  5.8 0.0 copy-done.8
  5.8 0.0 copy-done.7
  5.9 0.0 copy-done.3
  5.9 0.0 copy-done.2
  5.9 0.0 copy-done.6
  5.9 47.7 %middle.1 = (f32[3,2048]{1,0:T(4,128)S(1)}, f32[20,2048]{1,0:T(8,128)S(1)}, bf16[8,48,128]{2,1,0:T(8,128)(2,1)S(1)}) custom-call(bf16[8,384,128]{2,1,0:T(8,128)(2,1)S(1)} %pieces.1.agg, f32[1,2048]{1,0:T(1,128)S(1)} %bitcast.4, bf16[3,2048]{1,0:T(4,128)(2,1)S(1)} %copy-done.2, bf16[3,2048]{1,0:T(4,128)(2,1)S(1)} %copy-done.3, f32[1,2048]{1,0:T(1,128)S(1)} %bitcast.5, ...), custom_call_target="tpu_custom_call" | custom-call | tf_op jit(solution)/shard_map/middle/pallas_call | solution.py:341
  53.6 0.0 copy-done.5
  53.6 0.0 copy-done.4
  53.6 0.0 copy-done
  53.6 3.6 %back.1 = (f32[3,4096]{1,0:T(4,128)}, f32[3,2048]{1,0:T(4,128)}, f32[20,2048]{1,0:T(8,128)}) custom-call(s32[1,8,32]{2,1,0:T(8,128)S(1)} %copy-done.4, s32[1,8,32]{2,1,0:T(8,128)S(1)} %copy-done.5, bf16[8,48,128]{2,1,0:T(8,128)(2,1)S(1)} %get-tuple-element.9.flux_ref, bf16[1,8,64,2048]{3,2,1,0:T(8,128)(2,1)S(1)} %copy-done, ...), custom_call_target="tpu_custom_call" | custom-call | tf_op jit(solution)/shard_map/back/pallas_call | solution.py:378
Async XLA Ops:
  0.6 52.9 %copy-start.5 = (s32[1,8,32]{2,1,0:T(8,128)S(1)}, s32[1,8,32]{2,1,0:T(8,128)}, u32[]{:S(2)}) copy-start(s32[1,8,32]{2,1,0:T(8,128)} %dst_hbm.3) | copy-start | bytes 3076
  0.6 52.9 %copy-start.4 = (s32[1,8,32]{2,1,0:T(8,128)S(1)}, s32[1,8,32]{2,1,0:T(8,128)}, u32[]{:S(2)}) copy-start(s32[1,8,32]{2,1,0:T(8,128)} %src_hbm.3) | copy-start | bytes 3076
  0.7 52.9 %copy-start = (bf16[1,8,64,2048]{3,2,1,0:T(8,128)(2,1)S(1)}, bf16[1,8,64,2048]{3,2,1,0:T(8,128)(2,1)}, u32[]{:S(2)}) copy-start(bf16[1,8,64,2048]{3,2,1,0:T(8,128)(2,1)} %w_ref.1) | copy-start | bytes 6291460
  0.7 5.2 %copy-start.1 = (s32[2048,6]{0,1:T(8,128)S(1)}, s32[2048,6]{0,1:T(8,128)}, u32[]{:S(2)}) copy-start(s32[2048,6]{0,1:T(8,128)} %param.21) | copy-start | bytes 147460
  0.7 5.2 %copy-start.8 = (f32[20]{0:T(128)S(1)}, f32[20]{0:T(128)}, u32[]{:S(2)}) copy-start(f32[20]{0:T(128)} %level_weights.1) | copy-start | bytes 244
  0.7 5.2 %copy-start.7 = (f32[2048]{0:T(1024)S(1)}, f32[2048]{0:T(1024)}, u32[]{:S(2)}) copy-start(f32[2048]{0:T(1024)} %param.19) | copy-start | bytes 24580
  0.7 5.2 %copy-start.3 = (bf16[3,2048]{1,0:T(4,128)(2,1)S(1)}, bf16[3,2048]{1,0:T(4,128)(2,1)}, u32[]{:S(2)}) copy-start(bf16[3,2048]{1,0:T(4,128)(2,1)} %ocean_state.1) | copy-start | bytes 36868
  0.7 5.2 %copy-start.2 = (bf16[3,2048]{1,0:T(4,128)(2,1)S(1)}, bf16[3,2048]{1,0:T(4,128)(2,1)}, u32[]{:S(2)}) copy-start(bf16[3,2048]{1,0:T(4,128)(2,1)} %ice_flux.1) | copy-start | bytes 36868
  0.7 5.2 %copy-start.6 = (f32[2048]{0:T(1024)S(1)}, f32[2048]{0:T(1024)}, u32[]{:S(2)}) copy-start(f32[2048]{0:T(1024)} %param.16) | copy-start | bytes 24580

commit v6 on v5

--- a/solution.py
+++ b/solution.py
@@ -118,16 +118,22 @@
             src_ref=src, dst_ref=dst, send_sem=send, recv_sem=got, device_id=device, device_id_type=MESH
         )
 
-    sib_copies = [copy(agg.at[2 * m + 1], sib.at[m], sib_s.at[m], sib_r.at[m], sibling) for m in range(3)]
-    sib_copies.append(copy(agg.at[7], sib.at[3], sib_s.at[3], sib_r.at[3], part(1)))
-    far1 = copy(comb.at[0], recv.at[0], far_s.at[0], far_r.at[0], part(2))
-    far2 = copy(comb.at[1], recv.at[1], far_s.at[1], far_r.at[1], part(4))
-    far3 = copy(comb.at[2], recv.at[2], far_s.at[2], far_r.at[2], part(2))
-    for m in reversed(range(4)):
-        sib_copies[m].start()
-
-    def wide(ref, n):
-        return ref[n].astype(F32)
+    half = agg.shape[1] // 2
+    halves = [slice(0, half), slice(half, 2 * half)]
+    to_core = [
+        [copy(agg.at[2 * m + 1, h], sib.at[m, h], sib_s.at[m, n], sib_r.at[m, n], part(1) if m == 3 else sibling) for m in range(4)]
+        for n, h in enumerate(halves)
+    ]
+    along = [
+        [copy(comb.at[d, h], recv.at[d, h], far_s.at[d, n], far_r.at[d, n], part(2)) for d in range(3)]
+        for n, h in enumerate(halves)
+    ]
+    for m in (3, 2, 1, 0):
+        for n in range(2):
+            to_core[n][m].start()
+
+    def wide(ref, i, n):
+        return ref[i, halves[n], :].astype(F32)
 
     first = levels - 16
     ice8[...] = jnp.zeros_like(ice8)
@@ -159,29 +165,34 @@
             counts[h * 128 : h * 128 + 128, lanes] = total
         return carry
 
-    lax.fori_loop(0, 5 * tiles // 16, count_cells, 0)
-    sib_copies[3].wait_recv()
-    sib_copies[2].wait_recv()
-    comb[2] = (wide(agg, 6) + wide(sib, 3) + jnp.where(core == 0, wide(sib, 2), 0.0)).astype(BF16)
-    far3.start()
-    sib_copies[1].wait_recv()
-    sib_copies[0].wait_recv()
-    comb[0] = (wide(agg, 2) + wide(sib, core)).astype(BF16)
-    far1.start()
-
-    lax.fori_loop(5 * tiles // 16, 5 * tiles // 8, count_cells, 0)
-    far3.wait_recv()
-    comb[1] = (wide(agg, 4) + wide(sib, 1 + core) + wide(recv, 2)).astype(BF16)
-    far2.start()
-    lax.fori_loop(5 * tiles // 8, tiles, count_cells, 0)
-
-    far1.wait_recv()
-    far2.wait_recv()
+    lax.fori_loop(0, tiles // 4, count_cells, 0)
+    for n in range(2):
+        to_core[n][3].wait_recv()
+        to_core[n][2].wait_recv()
+        far = wide(agg, 6, n) + wide(sib, 3, n) + jnp.where(core == 0, wide(sib, 2, n), 0.0)
+        comb[2, halves[n], :] = far.astype(BF16)
+        along[n][2].start()
+    lax.fori_loop(tiles // 4, tiles // 2, count_cells, 0)
+    for n in range(2):
+        to_core[n][1].wait_recv()
+        to_core[n][0].wait_recv()
+    for n in range(2):
+        along[n][2].wait_recv()
+        comb[1, halves[n], :] = (wide(agg, 4, n) + wide(sib, 1 + core, n) + wide(recv, 2, n)).astype(BF16)
+        along[n][1].start()
+    lax.fori_loop(tiles // 2, 3 * tiles // 4, count_cells, 0)
+    for n in range(2):
+        along[n][1].wait_recv()
+        comb[0, halves[n], :] = (wide(agg, 2, n) + wide(sib, core, n) + wide(recv, 1, n)).astype(BF16)
+        along[n][0].start()
+    lax.fori_loop(3 * tiles // 4, tiles, count_cells, 0)
+    for n in range(2):
+        along[n][0].wait_recv()
 
     is_surf = lax.broadcasted_iota(jnp.int32, (8, 128), 0) >= first
     def merge(t):
         rows = slice(t * ROWS, (t + 2) * ROWS)
-        total = agg[0, rows, :].astype(F32) + recv[0, rows, :].astype(F32) + recv[1, rows, :].astype(F32)
+        total = agg[0, rows, :].astype(F32) + recv[0, rows, :].astype(F32)
         total = total + jnp.where(core == 1, sib[0, rows, :].astype(F32), 0.0)
         for u in range(2):
             lanes = slice((t + u) * 128, (t + u + 1) * 128)
@@ -233,7 +244,7 @@
         flux_copies[o - 1].wait_recv()
         flux_out[o] = flux_recv[o - 1]
 
-    for one in sib_copies + [far1, far2, far3, to_prev, to_next] + col_copies + flux_copies:
+    for one in to_core[0] + to_core[1] + along[0] + along[1] + [to_prev, to_next] + col_copies + flux_copies:
         one.wait_send()
 
 
@@ -365,8 +376,8 @@
             pltpu.VMEM((near - 1, tiles * surf, 128), BF16),
             pltpu.VMEM((1, cells), F32),
             pltpu.VMEM((max(lev_n - 1, 1), 1, cells), F32),
-            dma((4,)), dma((4,)),
-            dma((3,)), dma((3,)),
+            dma((4, 2)), dma((4, 2)),
+            dma((3, 2)), dma((3, 2)),
             dma((2,)), dma((2,)),
             dma((3,)), dma((3,)),
             dma((near - 1,)), dma((near - 1,)),

time: 57.3 us -> 59.1 us (1.031)
  Pallas kernels: 56.3 us -> 58.2 us
    pallas_call x1, Pallas kernels: 47.7 us -> 49.5 us  [shards(): pl.pallas_call(functools.partial(middle_kernel, grp_n, dom_n, lev_n), out...]
where the time goes in v6:
time: 59.1 us; the launch traced here: 59 us
  Pallas kernels  58.2 us (98%)
  between operations  0.79 us (1%)
    pallas_call x1, Pallas kernels, shards(): pl.pallas_call(functools.partial(middle_kernel, grp_n, dom_n, lev_n), out...  49.5 us
    pallas_call x1, Pallas kernels, shards(): pl.pallas_call(forward_kernel, out_shape=jax.ShapeDtypeStruct((near, flat...  5.09 us
    pallas_call x1, Pallas kernels, shards(): pl.pallas_call(back_kernel, out_shape=[jax.ShapeDtypeStruct((surf, column...  3.57 us

profile of v6, /device:TPU:1, one launch (start us, length us, event | category | flops | bytes accessed | tf_op | source)
XLA Modules:
  0.0 59.0 jit_solution(5562298555599596970)
XLA Ops:
  0.6 0.0 copy-start.5
  0.6 0.0 copy-start.4
  0.7 0.0 copy-start
  0.7 0.0 copy-start.1
  0.7 0.0 copy-start.8
  0.7 0.0 copy-start.7
  0.7 0.0 copy-start.3
  0.7 0.0 copy-start.2
  0.7 0.0 copy-start.6
  0.7 5.1 %pieces.1.agg = bf16[8,384,128]{2,1,0:T(8,128)(2,1)S(1)} custom-call(s32[1,8,32]{2,1,0:T(8,128)} %src_hbm.3, s32[1,8,32]{2,1,0:T(8,128)} %dst_hbm.3, bf16[3,4096]{1,0:T(4,128)(2,1)} %surf_hbm.1, bf16[20,4096]{1,0:T(8,128)(2,1)} %lev_hbm.1, bf16[1,8,64,2048]{3,2,1,0:T(8,128)(2,1)} %w_ref.1), custom_call_target="tpu_custom_call" | custom-call | tf_op jit(solution)/shard_map/pieces/pallas_call | solution.py:329
  5.8 0.0 copy-done.1
  5.8 0.0 copy-done.8
  5.8 0.0 copy-done.7
  5.8 0.0 copy-done.3
  5.9 0.0 copy-done.2
  5.9 0.0 copy-done.6
  5.9 49.5 %middle.1 = (f32[3,2048]{1,0:T(4,128)S(1)}, f32[20,2048]{1,0:T(8,128)S(1)}, bf16[8,48,128]{2,1,0:T(8,128)(2,1)S(1)}) custom-call(bf16[8,384,128]{2,1,0:T(8,128)(2,1)S(1)} %pieces.1.agg, f32[1,2048]{1,0:T(1,128)S(1)} %bitcast.4, bf16[3,2048]{1,0:T(4,128)(2,1)S(1)} %copy-done.2, bf16[3,2048]{1,0:T(4,128)(2,1)S(1)} %copy-done.3, f32[1,2048]{1,0:T(1,128)S(1)} %bitcast.5, ...), custom_call_target="tpu_custom_call" | custom-call | tf_op jit(solution)/shard_map/middle/pallas_call | solution.py:352
  55.4 0.0 copy-done.5
  55.4 0.0 copy-done.4
  55.4 0.0 copy-done
  55.4 3.6 %back.1 = (f32[3,4096]{1,0:T(4,128)}, f32[3,2048]{1,0:T(4,128)}, f32[20,2048]{1,0:T(8,128)}) custom-call(s32[1,8,32]{2,1,0:T(8,128)S(1)} %copy-done.4, s32[1,8,32]{2,1,0:T(8,128)S(1)} %copy-done.5, bf16[8,48,128]{2,1,0:T(8,128)(2,1)S(1)} %get-tuple-element.9.flux_ref, bf16[1,8,64,2048]{3,2,1,0:T(8,128)(2,1)S(1)} %copy-done, ...), custom_call_target="tpu_custom_call" | custom-call | tf_op jit(solution)/shard_map/back/pallas_call | solution.py:389
Async XLA Ops:
  0.6 54.8 %copy-start.5 = (s32[1,8,32]{2,1,0:T(8,128)S(1)}, s32[1,8,32]{2,1,0:T(8,128)}, u32[]{:S(2)}) copy-start(s32[1,8,32]{2,1,0:T(8,128)} %dst_hbm.3) | copy-start | bytes 3076
  0.6 54.8 %copy-start.4 = (s32[1,8,32]{2,1,0:T(8,128)S(1)}, s32[1,8,32]{2,1,0:T(8,128)}, u32[]{:S(2)}) copy-start(s32[1,8,32]{2,1,0:T(8,128)} %src_hbm.3) | copy-start | bytes 3076
  0.7 54.8 %copy-start = (bf16[1,8,64,2048]{3,2,1,0:T(8,128)(2,1)S(1)}, bf16[1,8,64,2048]{3,2,1,0:T(8,128)(2,1)}, u32[]{:S(2)}) copy-start(bf16[1,8,64,2048]{3,2,1,0:T(8,128)(2,1)} %w_ref.1) | copy-start | bytes 6291460
  0.7 5.2 %copy-start.1 = (s32[2048,6]{0,1:T(8,128)S(1)}, s32[2048,6]{0,1:T(8,128)}, u32[]{:S(2)}) copy-start(s32[2048,6]{0,1:T(8,128)} %param.21) | copy-start | bytes 147460
  0.7 5.2 %copy-start.8 = (f32[20]{0:T(128)S(1)}, f32[20]{0:T(128)}, u32[]{:S(2)}) copy-start(f32[20]{0:T(128)} %level_weights.1) | copy-start | bytes 244
  0.7 5.2 %copy-start.7 = (f32[2048]{0:T(1024)S(1)}, f32[2048]{0:T(1024)}, u32[]{:S(2)}) copy-start(f32[2048]{0:T(1024)} %param.19) | copy-start | bytes 24580
  0.7 5.2 %copy-start.3 = (bf16[3,2048]{1,0:T(4,128)(2,1)S(1)}, bf16[3,2048]{1,0:T(4,128)(2,1)}, u32[]{:S(2)}) copy-start(bf16[3,2048]{1,0:T(4,128)(2,1)} %ocean_state.1) | copy-start | bytes 36868
  0.7 5.2 %copy-start.2 = (bf16[3,2048]{1,0:T(4,128)(2,1)S(1)}, bf16[3,2048]{1,0:T(4,128)(2,1)}, u32[]{:S(2)}) copy-start(bf16[3,2048]{1,0:T(4,128)(2,1)} %ice_flux.1) | copy-start | bytes 36868
  0.7 5.2 %copy-start.6 = (f32[2048]{0:T(1024)S(1)}, f32[2048]{0:T(1024)}, u32[]{:S(2)}) copy-start(f32[2048]{0:T(1024)} %param.16) | copy-start | bytes 24580

commit v7 on v5

--- a/solution.py
+++ b/solution.py
@@ -19,11 +19,11 @@
     return jnp.dot(a, b, preferred_element_type=F32)
 
 
-def forward_kernel(src_hbm, dst_hbm, surf_hbm, lev_hbm, w_hbm, out_ref, src, dst, surf_ref, lev_ref, w_ref, joint, blocks, even, odd, small, big):
+def forward_kernel(src_hbm, dst_hbm, surf_hbm, lev_hbm, w_hbm, out_ref, src, dst, surf_ref, lev_ref, w_ref, joint, blocks, sums, small, big):
     levels, surf = lev_ref.shape[0], surf_ref.shape[0]
     near, width, across = w_ref.shape
     slots = across // width
-    count = even.shape[0] - 1
+    tiles = sums.shape[0] - 1
     arriving = [
         pltpu.make_async_copy(here, there, small.at[n])
         for n, (here, there) in enumerate([(lev_hbm, lev_ref), (surf_hbm, surf_ref), (src_hbm.at[0], src), (dst_hbm.at[0], dst)])
@@ -42,29 +42,24 @@
         blocks[2 * pair + 1] = both[:, 64:]
     arriving[2].wait()
     arriving[3].wait()
-    low = lax.broadcasted_iota(jnp.int32, (ROWS, 128), 1) < 64
+    side = lax.broadcasted_iota(jnp.int32, (ROWS, 128), 1) >> 6
 
     def offset(o, carry):
         pltpu.make_async_copy(w_hbm.at[0, o], w_ref.at[o], big.at[o]).wait()
-        even[...] = jnp.zeros_like(even)
-        odd[...] = jnp.zeros_like(odd)
+        sums[...] = jnp.zeros_like(sums)
         for pair in range(slots // 2):
-            a, b = 2 * pair, 2 * pair + 1
-            lhs = jnp.concatenate([blocks[src[o, a]], blocks[src[o, b]]], axis=0)
-            got = dot(lhs, w_ref[o, :, pair * 128 : pair * 128 + 128]).astype(BF16).astype(F32)
-            to_a, to_b = dst[o, a], dst[o, b]
-            to_a = jnp.where(to_a < 0, count, to_a)
-            to_b = jnp.where(to_b < 0, count, to_b)
-            even[to_a] = even[to_a] + got[:ROWS]
-            odd[to_b] = odd[to_b] + got[32 : 32 + ROWS]
-
-        def joined(t):
-            left = even[2 * t] + pltpu.roll(odd[2 * t], 64, 1)
-            right = pltpu.roll(even[2 * t + 1], 64, 1) + odd[2 * t + 1]
-            return jnp.where(low, left, right)
-
-        for t in range(0, count // 2, 2):
-            both = jnp.concatenate([joined(t), joined(t + 1)], axis=0)
+            slot = 2 * pair
+            lhs = jnp.concatenate([blocks[src[o, slot]], blocks[src[o, slot + 1]]], axis=0)
+            got = dot(lhs, w_ref[o, :, pair * 128 : pair * 128 + 128])
+            for u in range(2):
+                to = dst[o, slot + u]
+                tile = jnp.where(to < 0, tiles, to >> 1)
+                to_side = to & 1
+                one = got[32 * u : 32 * u + ROWS].astype(BF16).astype(F32)
+                one = pltpu.roll(one, 64 * (to_side ^ u), 1)
+                sums[tile] = sums[tile] + jnp.where(side == to_side, one, 0.0)
+        for t in range(0, tiles, 2):
+            both = jnp.concatenate([sums[t], sums[t + 1]], axis=0)
             out_ref[o, t * ROWS : (t + 2) * ROWS, :] = both.astype(BF16)
         return carry
 
@@ -328,8 +323,7 @@
             pltpu.VMEM((near, width, across), BF16),
             pltpu.VMEM((32, columns), F32),
             pltpu.VMEM((columns // width, 32, width), BF16),
-            pltpu.VMEM((cells // width + 1, ROWS, 128), F32),
-            pltpu.VMEM((cells // width + 1, ROWS, 128), F32),
+            pltpu.VMEM((tiles + 1, ROWS, 128), F32),
             dma((4,)),
             dma((near,)),
         ],

time: 57.3 us -> 57.4 us (level)
  no operation moved by 1% of the time
where the time goes in v7:
time: 57.4 us; the launch traced here: 57.2 us
  Pallas kernels  56.4 us (98%)
  between operations  0.79 us (1%)
    pallas_call x1, Pallas kernels, shards(): pl.pallas_call(functools.partial(middle_kernel, grp_n, dom_n, lev_n), out...  48.1 us
    pallas_call x1, Pallas kernels, shards(): pl.pallas_call(forward_kernel, out_shape=jax.ShapeDtypeStruct((near, flat...  4.75 us
    pallas_call x1, Pallas kernels, shards(): pl.pallas_call(back_kernel, out_shape=[jax.ShapeDtypeStruct((surf, column...  3.57 us

profile of v7, /device:TPU:1, one launch (start us, length us, event | category | flops | bytes accessed | tf_op | source)
XLA Modules:
  0.0 57.2 jit_solution(4634363204519317872)
XLA Ops:
  0.6 0.0 copy-start.5
  0.6 0.0 copy-start.4
  0.7 0.0 copy-start
  0.7 0.0 copy-start.1
  0.7 0.0 copy-start.8
  0.7 0.0 copy-start.7
  0.7 0.0 copy-start.3
  0.7 0.0 copy-start.2
  0.7 0.0 copy-start.6
  0.7 4.8 %pieces.1.agg = bf16[8,384,128]{2,1,0:T(8,128)(2,1)S(1)} custom-call(s32[1,8,32]{2,1,0:T(8,128)} %src_hbm.3, s32[1,8,32]{2,1,0:T(8,128)} %dst_hbm.3, bf16[3,4096]{1,0:T(4,128)(2,1)} %surf_hbm.1, bf16[20,4096]{1,0:T(8,128)(2,1)} %lev_hbm.1, bf16[1,8,64,2048]{3,2,1,0:T(8,128)(2,1)} %w_ref.1), custom_call_target="tpu_custom_call" | custom-call | tf_op jit(solution)/shard_map/pieces/pallas_call | solution.py:313
  5.5 0.0 copy-done.1
  5.5 0.0 copy-done.8
  5.5 0.0 copy-done.7
  5.5 0.0 copy-done.3
  5.5 0.0 copy-done.2
  5.5 0.0 copy-done.6
  5.5 48.1 %middle.1 = (f32[3,2048]{1,0:T(4,128)S(1)}, f32[20,2048]{1,0:T(8,128)S(1)}, bf16[8,48,128]{2,1,0:T(8,128)(2,1)S(1)}) custom-call(bf16[8,384,128]{2,1,0:T(8,128)(2,1)S(1)} %pieces.1.agg, f32[1,2048]{1,0:T(1,128)S(1)} %bitcast.4, bf16[3,2048]{1,0:T(4,128)(2,1)S(1)} %copy-done.2, bf16[3,2048]{1,0:T(4,128)(2,1)S(1)} %copy-done.3, f32[1,2048]{1,0:T(1,128)S(1)} %bitcast.5, ...), custom_call_target="tpu_custom_call" | custom-call | tf_op jit(solution)/shard_map/middle/pallas_call | solution.py:335
  53.6 0.0 copy-done.5
  53.6 0.0 copy-done.4
  53.6 0.0 copy-done
  53.6 3.6 %back.1 = (f32[3,4096]{1,0:T(4,128)}, f32[3,2048]{1,0:T(4,128)}, f32[20,2048]{1,0:T(8,128)}) custom-call(s32[1,8,32]{2,1,0:T(8,128)S(1)} %copy-done.4, s32[1,8,32]{2,1,0:T(8,128)S(1)} %copy-done.5, bf16[8,48,128]{2,1,0:T(8,128)(2,1)S(1)} %get-tuple-element.9.flux_ref, bf16[1,8,64,2048]{3,2,1,0:T(8,128)(2,1)S(1)} %copy-done, ...), custom_call_target="tpu_custom_call" | custom-call | tf_op jit(solution)/shard_map/back/pallas_call | solution.py:372
Async XLA Ops:
  0.6 53.0 %copy-start.5 = (s32[1,8,32]{2,1,0:T(8,128)S(1)}, s32[1,8,32]{2,1,0:T(8,128)}, u32[]{:S(2)}) copy-start(s32[1,8,32]{2,1,0:T(8,128)} %dst_hbm.3) | copy-start | bytes 3076
  0.6 53.0 %copy-start.4 = (s32[1,8,32]{2,1,0:T(8,128)S(1)}, s32[1,8,32]{2,1,0:T(8,128)}, u32[]{:S(2)}) copy-start(s32[1,8,32]{2,1,0:T(8,128)} %src_hbm.3) | copy-start | bytes 3076
  0.7 53.0 %copy-start = (bf16[1,8,64,2048]{3,2,1,0:T(8,128)(2,1)S(1)}, bf16[1,8,64,2048]{3,2,1,0:T(8,128)(2,1)}, u32[]{:S(2)}) copy-start(bf16[1,8,64,2048]{3,2,1,0:T(8,128)(2,1)} %w_ref.1) | copy-start | bytes 6291460
  0.7 4.8 %copy-start.1 = (s32[2048,6]{0,1:T(8,128)S(1)}, s32[2048,6]{0,1:T(8,128)}, u32[]{:S(2)}) copy-start(s32[2048,6]{0,1:T(8,128)} %param.21) | copy-start | bytes 147460
  0.7 4.8 %copy-start.8 = (f32[20]{0:T(128)S(1)}, f32[20]{0:T(128)}, u32[]{:S(2)}) copy-start(f32[20]{0:T(128)} %level_weights.1) | copy-start | bytes 244
  0.7 4.8 %copy-start.7 = (f32[2048]{0:T(1024)S(1)}, f32[2048]{0:T(1024)}, u32[]{:S(2)}) copy-start(f32[2048]{0:T(1024)} %param.19) | copy-start | bytes 24580
  0.7 4.8 %copy-start.3 = (bf16[3,2048]{1,0:T(4,128)(2,1)S(1)}, bf16[3,2048]{1,0:T(4,128)(2,1)}, u32[]{:S(2)}) copy-start(bf16[3,2048]{1,0:T(4,128)(2,1)} %ocean_state.1) | copy-start | bytes 36868
  0.7 4.8 %copy-start.2 = (bf16[3,2048]{1,0:T(4,128)(2,1)S(1)}, bf16[3,2048]{1,0:T(4,128)(2,1)}, u32[]{:S(2)}) copy-start(bf16[3,2048]{1,0:T(4,128)(2,1)} %ice_flux.1) | copy-start | bytes 36868
  0.7 4.8 %copy-start.6 = (f32[2048]{0:T(1024)S(1)}, f32[2048]{0:T(1024)}, u32[]{:S(2)}) copy-start(f32[2048]{0:T(1024)} %param.16) | copy-start | bytes 24580

commit v8 on v7

--- a/solution.py
+++ b/solution.py
@@ -113,16 +113,22 @@
             src_ref=src, dst_ref=dst, send_sem=send, recv_sem=got, device_id=device, device_id_type=MESH
         )
 
-    sib_copies = [copy(agg.at[2 * m + 1], sib.at[m], sib_s.at[m], sib_r.at[m], sibling) for m in range(3)]
-    sib_copies.append(copy(agg.at[7], sib.at[3], sib_s.at[3], sib_r.at[3], part(1)))
-    far1 = copy(comb.at[0], recv.at[0], far_s.at[0], far_r.at[0], part(2))
-    far2 = copy(comb.at[1], recv.at[1], far_s.at[1], far_r.at[1], part(4))
-    far3 = copy(comb.at[2], recv.at[2], far_s.at[2], far_r.at[2], part(2))
-    for m in reversed(range(4)):
-        sib_copies[m].start()
-
-    def wide(ref, n):
-        return ref[n].astype(F32)
+    half = agg.shape[1] // 2
+    halves = [slice(0, half), slice(half, 2 * half)]
+    to_core = [
+        [copy(agg.at[2 * m + 1, h], sib.at[m, h], sib_s.at[m, n], sib_r.at[m, n], part(1) if m == 3 else sibling) for m in range(4)]
+        for n, h in enumerate(halves)
+    ]
+    far1 = copy(comb.at[0], recv.at[0], far_s.at[0, 0], far_r.at[0, 0], part(2))
+    far2 = [copy(comb.at[1, h], recv.at[1, h], far_s.at[1, n], far_r.at[1, n], part(4)) for n, h in enumerate(halves)]
+    far3 = [copy(comb.at[2, h], recv.at[2, h], far_s.at[2, n], far_r.at[2, n], part(2)) for n, h in enumerate(halves)]
+    for ms in ((3, 2), (1, 0)):
+        for n in range(2):
+            for m in ms:
+                to_core[n][m].start()
+
+    def wide(ref, i, n):
+        return ref[i, halves[n], :].astype(F32)
 
     first = levels - 16
     ice8[...] = jnp.zeros_like(ice8)
@@ -155,23 +161,26 @@
         return carry
 
     lax.fori_loop(0, 5 * tiles // 16, count_cells, 0)
-    sib_copies[3].wait_recv()
-    sib_copies[2].wait_recv()
-    comb[2] = (wide(agg, 6) + wide(sib, 3) + jnp.where(core == 0, wide(sib, 2), 0.0)).astype(BF16)
-    far3.start()
-    sib_copies[1].wait_recv()
-    sib_copies[0].wait_recv()
-    comb[0] = (wide(agg, 2) + wide(sib, core)).astype(BF16)
+    for n in range(2):
+        to_core[n][3].wait_recv()
+        to_core[n][2].wait_recv()
+        far = wide(agg, 6, n) + wide(sib, 3, n) + jnp.where(core == 0, wide(sib, 2, n), 0.0)
+        comb[2, halves[n], :] = far.astype(BF16)
+        far3[n].start()
+    for n in range(2):
+        to_core[n][1].wait_recv()
+        to_core[n][0].wait_recv()
+        comb[0, halves[n], :] = (wide(agg, 2, n) + wide(sib, core, n)).astype(BF16)
     far1.start()
-
     lax.fori_loop(5 * tiles // 16, 5 * tiles // 8, count_cells, 0)
-    far3.wait_recv()
-    comb[1] = (wide(agg, 4) + wide(sib, 1 + core) + wide(recv, 2)).astype(BF16)
-    far2.start()
+    for n in range(2):
+        far3[n].wait_recv()
+        comb[1, halves[n], :] = (wide(agg, 4, n) + wide(sib, 1 + core, n) + wide(recv, 2, n)).astype(BF16)
+        far2[n].start()
     lax.fori_loop(5 * tiles // 8, tiles, count_cells, 0)
-
     far1.wait_recv()
-    far2.wait_recv()
+    far2[0].wait_recv()
+    far2[1].wait_recv()
 
     is_surf = lax.broadcasted_iota(jnp.int32, (8, 128), 0) >= first
     def merge(t):
@@ -228,7 +237,7 @@
         flux_copies[o - 1].wait_recv()
         flux_out[o] = flux_recv[o - 1]
 
-    for one in sib_copies + [far1, far2, far3, to_prev, to_next] + col_copies + flux_copies:
+    for one in to_core[0] + to_core[1] + far2 + far3 + [far1, to_prev, to_next] + col_copies + flux_copies:
         one.wait_send()
 
 
@@ -359,8 +368,8 @@
             pltpu.VMEM((near - 1, tiles * surf, 128), BF16),
             pltpu.VMEM((1, cells), F32),
             pltpu.VMEM((max(lev_n - 1, 1), 1, cells), F32),
-            dma((4,)), dma((4,)),
-            dma((3,)), dma((3,)),
+            dma((4, 2)), dma((4, 2)),
+            dma((3, 2)), dma((3, 2)),
             dma((2,)), dma((2,)),
             dma((3,)), dma((3,)),
             dma((near - 1,)), dma((near - 1,)),

time: 57.4 us -> 57.2 us (level)
  no operation moved by 1% of the time
where the time goes in v8:
time: 57.2 us; the launch traced here: 57 us
  Pallas kernels  56.2 us (98%)
  between operations  0.79 us (1%)
    pallas_call x1, Pallas kernels, shards(): pl.pallas_call(functools.partial(middle_kernel, grp_n, dom_n, lev_n), out...  47.9 us
    pallas_call x1, Pallas kernels, shards(): pl.pallas_call(forward_kernel, out_shape=jax.ShapeDtypeStruct((near, flat...  4.77 us
    pallas_call x1, Pallas kernels, shards(): pl.pallas_call(back_kernel, out_shape=[jax.ShapeDtypeStruct((surf, column...  3.57 us

profile of v8, /device:TPU:1, one launch (start us, length us, event | category | flops | bytes accessed | tf_op | source)
XLA Modules:
  0.0 57.0 jit_solution(16237314422727724060)
XLA Ops:
  0.6 0.0 copy-start.5
  0.6 0.0 copy-start.4
  0.7 0.0 copy-start
  0.7 0.0 copy-start.1
  0.7 0.0 copy-start.8
  0.7 0.0 copy-start.7
  0.7 0.0 copy-start.3
  0.7 0.0 copy-start.2
  0.7 0.0 copy-start.6
  0.7 4.8 %pieces.1.agg = bf16[8,384,128]{2,1,0:T(8,128)(2,1)S(1)} custom-call(s32[1,8,32]{2,1,0:T(8,128)} %src_hbm.3, s32[1,8,32]{2,1,0:T(8,128)} %dst_hbm.3, bf16[3,4096]{1,0:T(4,128)(2,1)} %surf_hbm.1, bf16[20,4096]{1,0:T(8,128)(2,1)} %lev_hbm.1, bf16[1,8,64,2048]{3,2,1,0:T(8,128)(2,1)} %w_ref.1), custom_call_target="tpu_custom_call" | custom-call | tf_op jit(solution)/shard_map/pieces/pallas_call | solution.py:322
  5.5 0.0 copy-done.1
  5.5 0.0 copy-done.8
  5.5 0.0 copy-done.7
  5.5 0.0 copy-done.3
  5.5 0.0 copy-done.2
  5.6 0.0 copy-done.6
  5.6 47.9 %middle.1 = (f32[3,2048]{1,0:T(4,128)S(1)}, f32[20,2048]{1,0:T(8,128)S(1)}, bf16[8,48,128]{2,1,0:T(8,128)(2,1)S(1)}) custom-call(bf16[8,384,128]{2,1,0:T(8,128)(2,1)S(1)} %pieces.1.agg, f32[1,2048]{1,0:T(1,128)S(1)} %bitcast.4, bf16[3,2048]{1,0:T(4,128)(2,1)S(1)} %copy-done.2, bf16[3,2048]{1,0:T(4,128)(2,1)S(1)} %copy-done.3, f32[1,2048]{1,0:T(1,128)S(1)} %bitcast.5, ...), custom_call_target="tpu_custom_call" | custom-call | tf_op jit(solution)/shard_map/middle/pallas_call | solution.py:344
  53.4 0.0 copy-done.5
  53.4 0.0 copy-done.4
  53.5 0.0 copy-done
  53.5 3.6 %back.1 = (f32[3,4096]{1,0:T(4,128)}, f32[3,2048]{1,0:T(4,128)}, f32[20,2048]{1,0:T(8,128)}) custom-call(s32[1,8,32]{2,1,0:T(8,128)S(1)} %copy-done.4, s32[1,8,32]{2,1,0:T(8,128)S(1)} %copy-done.5, bf16[8,48,128]{2,1,0:T(8,128)(2,1)S(1)} %get-tuple-element.9.flux_ref, bf16[1,8,64,2048]{3,2,1,0:T(8,128)(2,1)S(1)} %copy-done, ...), custom_call_target="tpu_custom_call" | custom-call | tf_op jit(solution)/shard_map/back/pallas_call | solution.py:381
Async XLA Ops:
  0.6 52.8 %copy-start.5 = (s32[1,8,32]{2,1,0:T(8,128)S(1)}, s32[1,8,32]{2,1,0:T(8,128)}, u32[]{:S(2)}) copy-start(s32[1,8,32]{2,1,0:T(8,128)} %dst_hbm.3) | copy-start | bytes 3076
  0.6 52.8 %copy-start.4 = (s32[1,8,32]{2,1,0:T(8,128)S(1)}, s32[1,8,32]{2,1,0:T(8,128)}, u32[]{:S(2)}) copy-start(s32[1,8,32]{2,1,0:T(8,128)} %src_hbm.3) | copy-start | bytes 3076
  0.7 52.8 %copy-start = (bf16[1,8,64,2048]{3,2,1,0:T(8,128)(2,1)S(1)}, bf16[1,8,64,2048]{3,2,1,0:T(8,128)(2,1)}, u32[]{:S(2)}) copy-start(bf16[1,8,64,2048]{3,2,1,0:T(8,128)(2,1)} %w_ref.1) | copy-start | bytes 6291460
  0.7 4.8 %copy-start.1 = (s32[2048,6]{0,1:T(8,128)S(1)}, s32[2048,6]{0,1:T(8,128)}, u32[]{:S(2)}) copy-start(s32[2048,6]{0,1:T(8,128)} %param.21) | copy-start | bytes 147460
  0.7 4.8 %copy-start.8 = (f32[20]{0:T(128)S(1)}, f32[20]{0:T(128)}, u32[]{:S(2)}) copy-start(f32[20]{0:T(128)} %level_weights.1) | copy-start | bytes 244
  0.7 4.8 %copy-start.7 = (f32[2048]{0:T(1024)S(1)}, f32[2048]{0:T(1024)}, u32[]{:S(2)}) copy-start(f32[2048]{0:T(1024)} %param.19) | copy-start | bytes 24580
  0.7 4.8 %copy-start.3 = (bf16[3,2048]{1,0:T(4,128)(2,1)S(1)}, bf16[3,2048]{1,0:T(4,128)(2,1)}, u32[]{:S(2)}) copy-start(bf16[3,2048]{1,0:T(4,128)(2,1)} %ocean_state.1) | copy-start | bytes 36868
  0.7 4.8 %copy-start.2 = (bf16[3,2048]{1,0:T(4,128)(2,1)S(1)}, bf16[3,2048]{1,0:T(4,128)(2,1)}, u32[]{:S(2)}) copy-start(bf16[3,2048]{1,0:T(4,128)(2,1)} %ice_flux.1) | copy-start | bytes 36868
  0.7 4.8 %copy-start.6 = (f32[2048]{0:T(1024)S(1)}, f32[2048]{0:T(1024)}, u32[]{:S(2)}) copy-start(f32[2048]{0:T(1024)} %param.16) | copy-start | bytes 24580

commit v9 on v7

--- a/solution.py
+++ b/solution.py
@@ -154,7 +154,7 @@
             counts[h * 128 : h * 128 + 128, lanes] = total
         return carry
 
-    lax.fori_loop(0, 5 * tiles // 16, count_cells, 0)
+    lax.fori_loop(0, tiles // 8, count_cells, 0)
     sib_copies[3].wait_recv()
     sib_copies[2].wait_recv()
     comb[2] = (wide(agg, 6) + wide(sib, 3) + jnp.where(core == 0, wide(sib, 2), 0.0)).astype(BF16)
@@ -164,11 +164,11 @@
     comb[0] = (wide(agg, 2) + wide(sib, core)).astype(BF16)
     far1.start()
 
-    lax.fori_loop(5 * tiles // 16, 5 * tiles // 8, count_cells, 0)
+    lax.fori_loop(tiles // 8, tiles // 4, count_cells, 0)
     far3.wait_recv()
     comb[1] = (wide(agg, 4) + wide(sib, 1 + core) + wide(recv, 2)).astype(BF16)
     far2.start()
-    lax.fori_loop(5 * tiles // 8, tiles, count_cells, 0)
+    lax.fori_loop(tiles // 4, tiles, count_cells, 0)
 
     far1.wait_recv()
     far2.wait_recv()

time: 57.4 us -> 57.4 us (level)
  no operation moved by 1% of the time
where the time goes in v9:
time: 57.4 us; the launch traced here: 57.2 us
  Pallas kernels  56.4 us (98%)
  between operations  0.79 us (1%)
    pallas_call x1, Pallas kernels, shards(): pl.pallas_call(functools.partial(middle_kernel, grp_n, dom_n, lev_n), out...  48.2 us
    pallas_call x1, Pallas kernels, shards(): pl.pallas_call(forward_kernel, out_shape=jax.ShapeDtypeStruct((near, flat...  4.66 us
    pallas_call x1, Pallas kernels, shards(): pl.pallas_call(back_kernel, out_shape=[jax.ShapeDtypeStruct((surf, column...  3.57 us

profile of v9, /device:TPU:1, one launch (start us, length us, event | category | flops | bytes accessed | tf_op | source)
XLA Modules:
  0.0 57.2 jit_solution(6398724632230706476)
XLA Ops:
  0.6 0.0 copy-start.5
  0.6 0.0 copy-start.4
  0.7 0.0 copy-start
  0.7 0.0 copy-start.1
  0.7 0.0 copy-start.8
  0.7 0.0 copy-start.7
  0.7 0.0 copy-start.3
  0.7 0.0 copy-start.2
  0.7 0.0 copy-start.6
  0.7 4.7 %pieces.1.agg = bf16[8,384,128]{2,1,0:T(8,128)(2,1)S(1)} custom-call(s32[1,8,32]{2,1,0:T(8,128)} %src_hbm.3, s32[1,8,32]{2,1,0:T(8,128)} %dst_hbm.3, bf16[3,4096]{1,0:T(4,128)(2,1)} %surf_hbm.1, bf16[20,4096]{1,0:T(8,128)(2,1)} %lev_hbm.1, bf16[1,8,64,2048]{3,2,1,0:T(8,128)(2,1)} %w_ref.1), custom_call_target="tpu_custom_call" | custom-call | tf_op jit(solution)/shard_map/pieces/pallas_call | solution.py:313
  5.4 0.0 copy-done.1
  5.4 0.0 copy-done.8
  5.4 0.0 copy-done.7
  5.4 0.0 copy-done.3
  5.4 0.0 copy-done.2
  5.4 0.0 copy-done.6
  5.4 48.2 %middle.1 = (f32[3,2048]{1,0:T(4,128)S(1)}, f32[20,2048]{1,0:T(8,128)S(1)}, bf16[8,48,128]{2,1,0:T(8,128)(2,1)S(1)}) custom-call(bf16[8,384,128]{2,1,0:T(8,128)(2,1)S(1)} %pieces.1.agg, f32[1,2048]{1,0:T(1,128)S(1)} %bitcast.4, bf16[3,2048]{1,0:T(4,128)(2,1)S(1)} %copy-done.2, bf16[3,2048]{1,0:T(4,128)(2,1)S(1)} %copy-done.3, f32[1,2048]{1,0:T(1,128)S(1)} %bitcast.5, ...), custom_call_target="tpu_custom_call" | custom-call | tf_op jit(solution)/shard_map/middle/pallas_call | solution.py:335
  53.6 0.0 copy-done.5
  53.7 0.0 copy-done.4
  53.7 0.0 copy-done
  53.7 3.6 %back.1 = (f32[3,4096]{1,0:T(4,128)}, f32[3,2048]{1,0:T(4,128)}, f32[20,2048]{1,0:T(8,128)}) custom-call(s32[1,8,32]{2,1,0:T(8,128)S(1)} %copy-done.4, s32[1,8,32]{2,1,0:T(8,128)S(1)} %copy-done.5, bf16[8,48,128]{2,1,0:T(8,128)(2,1)S(1)} %get-tuple-element.9.flux_ref, bf16[1,8,64,2048]{3,2,1,0:T(8,128)(2,1)S(1)} %copy-done, ...), custom_call_target="tpu_custom_call" | custom-call | tf_op jit(solution)/shard_map/back/pallas_call | solution.py:372
Async XLA Ops:
  0.6 53.0 %copy-start.5 = (s32[1,8,32]{2,1,0:T(8,128)S(1)}, s32[1,8,32]{2,1,0:T(8,128)}, u32[]{:S(2)}) copy-start(s32[1,8,32]{2,1,0:T(8,128)} %dst_hbm.3) | copy-start | bytes 3076
  0.6 53.0 %copy-start.4 = (s32[1,8,32]{2,1,0:T(8,128)S(1)}, s32[1,8,32]{2,1,0:T(8,128)}, u32[]{:S(2)}) copy-start(s32[1,8,32]{2,1,0:T(8,128)} %src_hbm.3) | copy-start | bytes 3076
  0.7 53.0 %copy-start = (bf16[1,8,64,2048]{3,2,1,0:T(8,128)(2,1)S(1)}, bf16[1,8,64,2048]{3,2,1,0:T(8,128)(2,1)}, u32[]{:S(2)}) copy-start(bf16[1,8,64,2048]{3,2,1,0:T(8,128)(2,1)} %w_ref.1) | copy-start | bytes 6291460
  0.7 4.7 %copy-start.1 = (s32[2048,6]{0,1:T(8,128)S(1)}, s32[2048,6]{0,1:T(8,128)}, u32[]{:S(2)}) copy-start(s32[2048,6]{0,1:T(8,128)} %param.21) | copy-start | bytes 147460
  0.7 4.7 %copy-start.8 = (f32[20]{0:T(128)S(1)}, f32[20]{0:T(128)}, u32[]{:S(2)}) copy-start(f32[20]{0:T(128)} %level_weights.1) | copy-start | bytes 244
  0.7 4.7 %copy-start.7 = (f32[2048]{0:T(1024)S(1)}, f32[2048]{0:T(1024)}, u32[]{:S(2)}) copy-start(f32[2048]{0:T(1024)} %param.19) | copy-start | bytes 24580
  0.7 4.7 %copy-start.3 = (bf16[3,2048]{1,0:T(4,128)(2,1)S(1)}, bf16[3,2048]{1,0:T(4,128)(2,1)}, u32[]{:S(2)}) copy-start(bf16[3,2048]{1,0:T(4,128)(2,1)} %ocean_state.1) | copy-start | bytes 36868
  0.7 4.7 %copy-start.2 = (bf16[3,2048]{1,0:T(4,128)(2,1)S(1)}, bf16[3,2048]{1,0:T(4,128)(2,1)}, u32[]{:S(2)}) copy-start(bf16[3,2048]{1,0:T(4,128)(2,1)} %ice_flux.1) | copy-start | bytes 36868
  0.7 4.7 %copy-start.6 = (f32[2048]{0:T(1024)S(1)}, f32[2048]{0:T(1024)}, u32[]{:S(2)}) copy-start(f32[2048]{0:T(1024)} %param.16) | copy-start | bytes 24580
